TPU v7x, 256 devices: a whole 4x4x8 slice. The times are simulated.
256 devices in a mesh: lon: 8 (over z), lat: 16 (over y, x), lev: 2 (over core).
Axes of the slice: x: 4, y: 4, z: 8, core: 2. Of those that a mesh axis runs over, the one named last changes fastest.
Arguments:
- ensemble: float32 [80, 3, 2, 256, 1024], P(None, None, 'lev', 'lat', 'lon'), may hold values from -6 to 6
- courant: float32 [2, 2, 256, 1024], P(None, 'lev', 'lat', 'lon'), may hold values from -0.6 to 0.6
- obs_value: float32 [2, 256], replicated, may hold values from -6 to 6
- obs_error: float32 [2, 256], replicated, may hold values from 0.25 to 4
- owner_device: int32 [2], replicated, may hold values from 0 to 255
- columns: int32 [2, 256], replicated, may hold values from 0 to 2047
Outputs:
- analysis: float32 [80, 3, 2, 256, 1024], P(None, None, 'lev', 'lat', 'lon')
Inputs may be any that keep to these rules, and one draw needn't show every extreme that they name: `owner_device`: devices are counted over lon, lat and lev with lev fastest; all observations of a batch lie on the owner's level and observe the first field. `columns`: A column index counts the owner's cells row by row of 128 longitudes; two observations may share a column.
All inputs are finite; a program needn't handle non-finite values.
Results may differ from a plain program's by a relative error of at most 0.0003.
Values sent between devices are 32-bit elements; how exact they have to be, the bound alone decides.
A program may use at most 128 MiB of HBM per device.

v0:
```python
import jax
import jax.numpy as jnp
from jax import lax
from jax.sharding import PartitionSpec as P

CY = 16


PLUS_WEIGHTS = (-2.0, 15.0, -60.0, 20.0, 30.0, -3.0)
MINUS_WEIGHTS = (3.0, -30.0, -20.0, 60.0, -15.0, 2.0)


def from_root(block, axis, source):
    block = jnp.where(lax.axis_index(axis) == source, block, jnp.zeros_like(block))
    return lax.psum(block, axis)


def padded_2(x, sides, width, wrap):
    for axis, dim in sides:
        size, length = (lax.axis_size(axis), x.shape[dim])
        up = [(i, (i + 1) % size) for i in range(size if wrap else size - 1)]
        down = [(j, i) for i, j in up]
        last = lax.slice_in_dim(x, length - width, length, axis=dim)
        initial = lax.slice_in_dim(x, 0, width, axis=dim)
        before = lax.ppermute(last, axis, up)
        after = lax.ppermute(initial, axis, down)
        x = jnp.concatenate([before, x, after], axis=dim)
    return x


def upwind(padded, along_axis, length_out):
    plus_sum = PLUS_WEIGHTS[0] * lax.slice_in_dim(padded, 0, length_out, axis=along_axis)
    minus_sum = MINUS_WEIGHTS[0] * lax.slice_in_dim(padded, 1, 1 + length_out, axis=along_axis)
    for offset_index in range(1, 6):
        plus_sum = plus_sum + PLUS_WEIGHTS[offset_index] * lax.slice_in_dim(
            padded, offset_index, offset_index + length_out, axis=along_axis
        )
        minus_sum = minus_sum + MINUS_WEIGHTS[offset_index] * lax.slice_in_dim(
            padded, offset_index + 1, offset_index + 1 + length_out, axis=along_axis
        )
    return (plus_sum / 60.0, minus_sum / 60.0)


def combine(plus_lon, minus_lon, plus_lat, minus_lat, east_courant, north_courant):
    lon_term = (
        jnp.maximum(east_courant, 0.0) * plus_lon + jnp.minimum(east_courant, 0.0) * minus_lon
    )
    lat_term = (
        jnp.maximum(north_courant, 0.0) * plus_lat + jnp.minimum(north_courant, 0.0) * minus_lat
    )
    return -(lon_term + lat_term)


def innovation_terms(obs_prior, observed, obs_err):
    members = obs_prior.shape[0]
    centre = jnp.mean(obs_prior, axis=0)
    obs_spread = obs_prior - centre
    variance = jnp.sum(obs_spread * obs_spread, axis=0) / (members - 1)
    denominator = variance + obs_err
    factor = 1.0 / (1.0 + jnp.sqrt(obs_err / denominator))
    gain_matrix = (observed - centre - factor * obs_spread) / denominator
    return (obs_spread, gain_matrix)


def taper_tile(obs_rows, obs_cols, grid_rows, grid_cols, lon_total):
    dlat = (grid_rows[None, :, None] - obs_rows[:, None, None]).astype(jnp.float32)
    lon_gap = jnp.abs(grid_cols[None, None, :] - obs_cols[:, None, None])
    lon_gap = jnp.minimum(lon_gap, lon_total - lon_gap).astype(jnp.float32)
    ratio = jnp.sqrt((dlat / (2.0 * CY)) ** 2 + (lon_gap / (1.0 * (lon_total // 2))) ** 2)
    inner = -(ratio**5) / 4.0 + ratio**4 / 2.0 + 5.0 * ratio**3 / 8.0 - 5.0 * ratio**2 / 3.0 + 1.0
    safe = jnp.maximum(ratio, 1.0)
    outer = (
        safe**5 / 12.0
        - safe**4 / 2.0
        + 5.0 * safe**3 / 8.0
        + 5.0 * safe**2 / 3.0
        - 5.0 * safe
        + 4.0
        - 2.0 / (3.0 * safe)
    )
    return jnp.where(ratio <= 1.0, inner, jnp.where(ratio < 2.0, outer, 0.0))


def local_taper(owner, column_ids, lat_rows, lon_cols):
    lat_count = lax.axis_size("lat")
    lev_count = lax.axis_size("lev")
    lon_index = owner // (lat_count * lev_count)
    lat_index = owner // lev_count % lat_count
    obs_rows = lat_index * lat_rows + column_ids // lon_cols
    obs_cols = lon_index * lon_cols + column_ids % lon_cols
    grid_rows = lax.axis_index("lat") * lat_rows + jnp.arange(lat_rows, dtype=jnp.int32)
    grid_cols = lax.axis_index("lon") * lon_cols + jnp.arange(lon_cols, dtype=jnp.int32)
    tile = taper_tile(obs_rows, obs_cols, grid_rows, grid_cols, lon_cols * lax.axis_size("lon"))
    return tile.reshape(tile.shape[0], lat_rows * lon_cols)


def share_prior(candidate, root_device):
    return from_root(candidate, ("lon", "lat", "lev"), root_device)


def regress_all(state_flat, anomaly, obs_spread, gain_matrix, weights):
    members, field_count, cell_count = state_flat.shape
    covariance = jnp.dot(
        obs_spread.T,
        anomaly.reshape(members, field_count * cell_count),
        precision=lax.Precision.HIGHEST,
    ) / (members - 1)
    weighted = weights[:, None, :] * covariance.reshape(-1, field_count, cell_count)
    change = jnp.dot(
        gain_matrix, weighted.reshape(-1, field_count * cell_count), precision=lax.Precision.HIGHEST
    )
    return state_flat + change.reshape(members, field_count, cell_count)


def regress(state_flat, anomaly, obs_spread, gain_matrix, weights):
    return regress_all(state_flat, anomaly, obs_spread, gain_matrix, weights)


def rim_tendency(values, east_courant, north_courant):
    lon_padded = padded_2(values, (("lon", 3),), 3, True)
    lat_padded = padded_2(values, (("lat", 2),), 3, False)
    plus_lon, minus_lon = upwind(lon_padded, 3, values.shape[3])
    plus_lat, minus_lat = upwind(lat_padded, 2, values.shape[2])
    return combine(plus_lon, minus_lon, plus_lat, minus_lat, east_courant, north_courant)


def on_device(ensemble, courant, obs_value, obs_error, owner_device, columns):
    members = ensemble.shape[0]
    field_count = ensemble.shape[1]
    lat_rows = ensemble.shape[3]
    lon_cols = ensemble.shape[4]
    cell_count = lat_rows * lon_cols
    batch_count = columns.shape[0]
    state_flat = ensemble.reshape(members, field_count, cell_count)
    obs_prior = share_prior(jnp.take(state_flat[:, 0], columns[0], axis=1), owner_device[0])
    for batch_index in range(batch_count):
        obs_spread, gain_matrix = innovation_terms(
            obs_prior, obs_value[batch_index], obs_error[batch_index]
        )
        weights = local_taper(owner_device[batch_index], columns[batch_index], lat_rows, lon_cols)
        anomaly = state_flat - jnp.mean(state_flat, axis=0)
        state_flat = regress(state_flat, anomaly, obs_spread, gain_matrix, weights)
        if batch_index + 1 < batch_count:
            obs_prior = share_prior(
                jnp.take(state_flat[:, 0], columns[batch_index + 1], axis=1),
                owner_device[batch_index + 1],
            )
    fields = state_flat.reshape(members * field_count, 1, lat_rows, lon_cols)
    east_courant = courant[0]
    north_courant = courant[1]
    section_one = fields + rim_tendency(fields, east_courant, north_courant) / 3.0
    section_two = fields + rim_tendency(section_one, east_courant, north_courant) / 2.0
    advected = fields + rim_tendency(section_two, east_courant, north_courant)
    return advected.reshape(ensemble.shape)


def solution(mesh):
    return jax.shard_map(
        on_device,
        mesh=mesh,
        in_specs=(
            P(None, None, "lev", "lat", "lon"),
            P(None, "lev", "lat", "lon"),
            P(),
            P(),
            P(),
            P(),
        ),
        out_specs=P(None, None, "lev", "lat", "lon"),
        check_vma=False,
    )
```

profile of v0, /device:TPU:8, one launch (start us, length us, event | category | flops | bytes accessed | tf_op | source)
XLA Modules:
  0.0 713.3 jit_solution(12419167702578340365)
XLA Ops:
  25.8 3.5 fusion.18
  29.5 4.6 fusion.36
  34.8 4.7 mul.548
  39.5 6.5 copy.28
  46.0 4.7 mul.565
  50.8 6.6 copy.33
  57.3 210.8 %all-reduce.3.cloned.1.call-done = f32[80,256]{0,1:T(8,128)} async-done(((f32[80,256]{0,1:T(8,128)}), f32[80,256]{0,1:T(8,128)}) %all-reduce.3.cloned.1.call-update) | async-done | bytes 81936 | tf_op jit(solution)/shard_map/psum | solution.py:15
  269.1 9.6 %fusion.3 = f32[6144,256]{0,1:T(8,128)} fusion(f32[256,6144]{1,0:T(8,128)} %copy.28, f32[10,8,48,128]{3,2,1,0:T(8,128)S(1)} %bitcast.85, f32[6144]{0:T(1024)S(1)} %bitcast.87, f32[80,256]{0,1:T(8,128)} %all-reduce.3.cloned.1.call-done, f32[256]{0:T(256)S(1)} %broadcast_multiply_fusion.5), kind=kOutput, calls=%fused_computation.7 | convolution fusion | flops 1513607168 | bytes 14656512 | tf_op jit(solution)/shard_map/dot_general | solution.py:103
  278.7 6.8 copy.29
  285.8 9.9 %fusion.188 = (f32[3,2048]{1,0:T(4,128)S(1)}, f32[80,3,2048]{2,0,1:T(8,128)S(1)}) fusion(f32[80,3,2048]{2,0,1:T(8,128)} %copy-done.3, f32[3,2048,256]{2,1,0:T(8,128)} %bitcast.81, f32[80,256]{0,1:T(8,128)S(1)} %copy-done.4, f32[256]{0:T(256)S(1)} %bitcast.95, f32[256]{0:T(256)S(1)} %bitcast.94, f32[256]{0:T(256)S(1)} %broadcast_multiply_fusion.5, ...), kind=kOutput, calls=%fused_computation.324 | convolution fusion | flops 1511008256 | bytes 10334208 | tf_op jit(solution)/shard_map/dot_general | solution.py:109
  301.1 236.9 %all-reduce.5.cloned.1.call-done = f32[80,256]{0,1:T(8,128)} async-done(((f32[80,256]{0,1:T(8,128)}), f32[80,256]{0,1:T(8,128)}) %all-reduce.5.cloned.1.call-update) | async-done | bytes 81936 | tf_op jit(solution)/shard_map/psum | solution.py:15
  540.1 9.4 %fusion.1 = f32[6144,256]{0,1:T(8,128)} fusion(f32[256,6144]{1,0:T(8,128)} %copy.33, f32[80,6144]{1,0:T(8,128)} %bitcast.86, f32[80,256]{0,1:T(8,128)} %all-reduce.5.cloned.1.call-done, f32[256]{0:T(256)S(1)} %broadcast_multiply_fusion.4), kind=kOutput, calls=%fused_computation.4 | convolution fusion | flops 1513115648 | bytes 14631936 | tf_op jit(solution)/shard_map/dot_general | solution.py:103
  549.5 6.6 copy.34
  556.1 8.9 %convolution_add_fusion = f32[80,3,2048]{2,0,1:T(8,128)S(1)} fusion(f32[80,3,2048]{2,0,1:T(8,128)S(1)} %get-tuple-element.41, f32[3,2048,256]{2,1,0:T(8,128)} %bitcast.82, f32[80,256]{0,1:T(8,128)S(1)} %copy-done.5, f32[256]{0:T(256)S(1)} %bitcast.93, f32[256]{0:T(256)S(1)} %bitcast.92, f32[256]{0:T(256)S(1)} %broadcast_multiply_fusion.4, f32[256]{0:T(256)S(1)} %bitcast.91), kind=kOutput, calls=%fused_computation.72 | convolution fusion | flops 1510522880 | bytes 10309632 | tf_op jit(solution)/shard_map/dot_general | solution.py:109
  567.9 3.3 reshape.508
  572.1 4.3 collective-permute-start.3
  586.4 3.2 collective-permute-start.1
  598.2 13.2 %fusion.92 = f32[240,1,16,128]{3,2,0,1:T(8,128)S(1)} fusion(f32[240,1,16,128]{3,2,0,1:T(8,128)S(1)} %reshape.508, f32[240,1,3,128]{3,2,0,1:T(4,128)S(1)} %collective-permute-done.2, f32[240,1,16,3]{3,2,0,1:T(8,128)} %copy.38, f32[240,1,19,128]{3,2,0,1:T(8,128)} %constant_dynamic-update-slice_fusion, f32[240,1,16,3]{3,2,0,1:T(8,128)} %copy.40, ...), kind=kLoop, calls=%fused_computation.164 | loop fusion | flops 29982720 | bytes 10323968 | tf_op jit(solution)/shard_map/add | solution.py:151
  613.5 6.0 collective-permute-start.7
  627.7 3.2 collective-permute-start.5
  637.0 21.5 %fusion.78 = f32[240,1,16,128]{3,2,0,1:T(8,128)S(1)} fusion(f32[240,1,16,128]{3,2,0,1:T(8,128)S(1)} %reshape.508, f32[240,1,16,128]{3,2,0,1:T(8,128)} %copy-done, f32[240,1,3,128]{3,2,0,1:T(4,128)S(1)} %collective-permute-done.6, f32[240,1,16,3]{3,2,0,1:T(8,128)} %copy.42, f32[240,1,3,128]{3,2,0,1:T(4,128)} %collective-permute-done.7, ...), kind=kLoop, calls=%fused_computation.150 | loop fusion | flops 31457280 | bytes 6760448 | tf_op jit(solution)/shard_map/add | solution.py:152
  660.7 6.0 collective-permute-start.11
  674.9 3.2 collective-permute-start.9
  684.3 21.9 %fusion.62 = f32[240,1,16,128]{3,2,0,1:T(8,128)} fusion(f32[240,1,16,128]{3,2,0,1:T(8,128)S(1)} %reshape.508, f32[240,1,16,128]{3,2,0,1:T(8,128)} %copy-done.1, f32[240,1,3,128]{3,2,0,1:T(4,128)S(1)} %collective-permute-done.10, f32[240,1,16,3]{3,2,0,1:T(8,128)} %copy.46, f32[240,1,3,128]{3,2,0,1:T(4,128)} %collective-permute-done.11, ...), kind=kLoop, calls=%fused_computation.134 | loop fusion | flops 30965760 | bytes 6760448 | tf_op jit(solution)/shard_map/add | solution.py:153
  (101 shorter events, 77.6 us)
Async XLA Ops:
  6.5 261.6 %all-reduce.3.cloned.1.call-start = ((), (), s32[]{:S(2)}) async-start(), calls=%async_computation | async-start | bytes 262144 | tf_op jit(solution)/shard_map/psum | solution.py:15
  18.4 4.6 copy-start.3
  23.0 514.9 %all-reduce.5.cloned.1.call-start = ((), (), s32[]{:S(2)}) async-start(), calls=%async_computation.1 | async-start | bytes 262144 | tf_op jit(solution)/shard_map/psum | solution.py:15
  25.8 3.5 copy-start.2
  29.5 4.6 copy-start.6
  278.7 6.8 copy-start.4
  278.7 7.0 copy-start.8
  278.7 7.0 copy-start.7
  549.5 6.6 copy-start.5
  572.1 25.1 %collective-permute-start.3 = (f32[240,1,3,128]{3,2,0,1:T(4,128)}, f32[240,1,3,128]{3,2,0,1:T(4,128)S(1)}, u32[]{:S(2)}, u32[]{:S(2)}) collective-permute-start(f32[240,1,3,128]{3,2,0,1:T(4,128)} %get-tuple-element.20), channel_id=1, source_target_pairs={{2,0},{4,2},{6,4},{8,6},{10,8},{12,10},{14,12},{16,14},{18,16},{20... | collective-permute-start | bytes 1105928 | tf_op jit(solution)/shard_map/ppermute | solution.py:26
  576.4 21.8 %collective-permute-start.2 = (f32[240,1,3,128]{3,2,0,1:T(4,128)S(1)}, f32[240,1,3,128]{3,2,0,1:T(4,128)S(1)}, u32[]{:S(2)}, u32[]{:S(2)}) collective-permute-start(f32[240,1,3,128]{3,2,0,1:T(4,128)S(1)} %get-tuple-element.21), channel_id=1, source_target_pairs={{0,2},{2,4},{4,6},{6,8},{8,10},{10,12},{12,14},{14,16},{16,18},{18... | collective-permute-start | bytes 1105928 | tf_op jit(solution)/shard_map/ppermute | solution.py:25
  583.3 7.8 %collective-permute-start = (f32[240,1,16,3]{0,2,3,1:T(8,128)S(1)}, f32[240,1,16,3]{0,2,3,1:T(8,128)}, u32[]{:S(2)}, u32[]{:S(2)}) collective-permute-start(f32[240,1,16,3]{0,2,3,1:T(8,128)S(1)} %copy.37), channel_id=1, source_target_pairs={{0,32},{32,64},{64,96},{96,128},{128,160},{160,192},{192,224},{224... | collective-permute-start | bytes 138248 | tf_op jit(solution)/shard_map/ppermute | solution.py:25
  586.4 7.8 %collective-permute-start.1 = (f32[240,1,16,3]{0,2,3,1:T(8,128)}, f32[240,1,16,3]{0,2,3,1:T(8,128)}, u32[]{:S(2)}, u32[]{:S(2)}) collective-permute-start(f32[240,1,16,3]{0,2,3,1:T(8,128)} %copy.39), channel_id=1, source_target_pairs={{32,0},{64,32},{96,64},{128,96},{160,128},{192,160},{224,192},{0,2... | collective-permute-start | bytes 138248 | tf_op jit(solution)/shard_map/ppermute | solution.py:26
  611.4 10.7 %copy-start = (f32[240,1,16,128]{3,2,0,1:T(8,128)}, f32[240,1,16,128]{3,2,0,1:T(8,128)S(1)}, u32[]{:S(2)}) copy-start(f32[240,1,16,128]{3,2,0,1:T(8,128)S(1)} %fusion.92) | copy-start | bytes 5898244
  611.6 25.4 %collective-permute-start.6 = (f32[240,1,3,128]{3,2,0,1:T(4,128)S(1)}, f32[240,1,3,128]{3,2,0,1:T(4,128)S(1)}, u32[]{:S(2)}, u32[]{:S(2)}) collective-permute-start(f32[240,1,3,128]{3,2,0,1:T(4,128)S(1)} %get-tuple-element.17), channel_id=1, source_target_pairs={{0,2},{2,4},{4,6},{6,8},{8,10},{10,12},{12,14},{14,16},{16,18},{18... | collective-permute-start | bytes 1105928 | tf_op jit(solution)/shard_map/ppermute | solution.py:25
  613.5 23.5 %collective-permute-start.7 = (f32[240,1,3,128]{3,2,0,1:T(4,128)S(1)}, f32[240,1,3,128]{3,2,0,1:T(4,128)}, u32[]{:S(2)}, u32[]{:S(2)}) collective-permute-start(f32[240,1,3,128]{3,2,0,1:T(4,128)S(1)} %get-tuple-element.16), channel_id=1, source_target_pairs={{2,0},{4,2},{6,4},{8,6},{10,8},{12,10},{14,12},{16,14},{18,16},{20... | collective-permute-start | bytes 1105928 | tf_op jit(solution)/shard_map/ppermute | solution.py:26
  624.6 6.3 collective-permute-start.4
  627.7 6.3 collective-permute-start.5
  658.5 10.7 %copy-start.1 = (f32[240,1,16,128]{3,2,0,1:T(8,128)}, f32[240,1,16,128]{3,2,0,1:T(8,128)S(1)}, u32[]{:S(2)}) copy-start(f32[240,1,16,128]{3,2,0,1:T(8,128)S(1)} %fusion.78) | copy-start | bytes 5898244
  658.7 25.6 %collective-permute-start.10 = (f32[240,1,3,128]{3,2,0,1:T(4,128)S(1)}, f32[240,1,3,128]{3,2,0,1:T(4,128)S(1)}, u32[]{:S(2)}, u32[]{:S(2)}) collective-permute-start(f32[240,1,3,128]{3,2,0,1:T(4,128)S(1)} %get-tuple-element.13), channel_id=1, source_target_pairs={{0,2},{2,4},{4,6},{6,8},{8,10},{10,12},{12,14},{14,16},{16,18},{18... | collective-permute-start | bytes 1105928 | tf_op jit(solution)/shard_map/ppermute | solution.py:25
  660.7 23.6 %collective-permute-start.11 = (f32[240,1,3,128]{3,2,0,1:T(4,128)S(1)}, f32[240,1,3,128]{3,2,0,1:T(4,128)}, u32[]{:S(2)}, u32[]{:S(2)}) collective-permute-start(f32[240,1,3,128]{3,2,0,1:T(4,128)S(1)} %get-tuple-element.12), channel_id=1, source_target_pairs={{2,0},{4,2},{6,4},{8,6},{10,8},{12,10},{14,12},{16,14},{18,16},{20... | collective-permute-start | bytes 1105928 | tf_op jit(solution)/shard_map/ppermute | solution.py:26
  671.7 6.5 collective-permute-start.8
  674.9 6.3 collective-permute-start.9
Sparse Core Ops, SparseCore 0:
  23.2 244.9 all-reduce.2
  299.6 238.3 all-reduce.4
where the time goes:
time: 722 us; the launch traced here: 713 us
  waiting for transfers between devices  448 us (62%)
  local copies, waits for them, and re-layouts  103 us (14%)
  other arithmetic  72.7 us (10%)
  matrix products  37.8 us (5%)
  starting transfers between devices  32.1 us (4%)
  between operations  20.4 us (3%)
    psum x2, waiting for transfers between devices, from_root(): return lax.psum(block, axis)  448 us
    ppermute x6, starting transfers between devices, padded_2(): after = lax.ppermute(initial, axis, down)  26 us
    mul x4, local copies, waits for them, and re-layouts, regress_all(): weights[:, None, :] * covariance.reshape(-1, field_count, cell_count)  22.6 us
    add x1, other arithmetic, on_device(): advected = fields + rim_tendency(section_two, east_courant, north_courant)  21.9 us
    add x1, other arithmetic, on_device(): fields + rim_tendency(section_one, east_courant, north_courant) / 2.0  21.5 us
    dot_general x2, matrix products, regress_all(): jnp.dot(obs_spread.T, anomaly.reshape(members, field_count * cell_count),...  19 us
    dot_general x2, matrix products, regress_all(): jnp.dot(gain_matrix, weighted.reshape(-1, field_count * cell_count), prec...  18.8 us
    slice x9, local copies, waits for them, and re-layouts, padded_2(): initial = lax.slice_in_dim(x, 0, width, axis=dim)  18 us
  transfers between devices with their start and end apart: 14, of which 2 were waited for; matrix products, arithmetic and copies ran while one was open for 11% of the time, Pallas kernels for 0%

commit v1 on v0

v1 whole, which is shorter than its diff:
```python
import functools

import jax
import jax.numpy as jnp
from jax import lax
from jax.experimental import pallas as pl
from jax.experimental.pallas import tpu as pltpu
from jax.sharding import PartitionSpec as P

MESH = pl.DeviceIdType.MESH
PLUS_WEIGHTS = (-2.0, 15.0, -60.0, 20.0, 30.0, -3.0)
MINUS_WEIGHTS = (3.0, -30.0, -20.0, 60.0, -15.0, 2.0)
VMEM_LIMIT = 60 * 1024 * 1024


def share_kernel(n_lon, n_lat, n_lev, cand, out, rs_buf, z_buf, send_sems, recv_sems):
    lon = lax.axis_index("lon")
    lat = lax.axis_index("lat")
    lev = lax.axis_index("lev")
    group = n_lat * n_lev
    me = lat * n_lev + lev

    def wait_all(buf, count, sem):
        view = buf.at[pl.ds(0, count)]
        pltpu.make_async_copy(view, view, sem).wait()

    def send_piece(t, carry):
        other = lax.rem(me + t, group)
        pltpu.make_async_remote_copy(
            src_ref=cand.at[other],
            dst_ref=rs_buf.at[me],
            send_sem=send_sems.at[0],
            recv_sem=recv_sems.at[0],
            device_id=(lon, other // n_lev, lax.rem(other, n_lev)),
            device_id_type=MESH,
        ).start()
        return carry

    lax.fori_loop(1, group, send_piece, 0)
    rs_buf[me] = cand[me]
    wait_all(rs_buf, group - 1, recv_sems.at[0])
    z_buf[lon] = jnp.sum(rs_buf[...], axis=0)

    def send_sum(t, carry):
        other = lax.rem(lon + t, n_lon)
        pltpu.make_async_remote_copy(
            src_ref=z_buf.at[lon],
            dst_ref=z_buf.at[lon],
            send_sem=send_sems.at[1],
            recv_sem=recv_sems.at[1],
            device_id=(other, lat, lev),
            device_id_type=MESH,
        ).start()
        return carry

    lax.fori_loop(1, n_lon, send_sum, 0)
    wait_all(z_buf, n_lon - 1, recv_sems.at[1])
    out[me] = jnp.sum(z_buf[...], axis=0)

    def send_total(t, carry):
        other = lax.rem(me + t, group)
        pltpu.make_async_remote_copy(
            src_ref=out.at[me],
            dst_ref=out.at[me],
            send_sem=send_sems.at[2],
            recv_sem=recv_sems.at[2],
            device_id=(lon, other // n_lev, lax.rem(other, n_lev)),
            device_id_type=MESH,
        ).start()
        return carry

    lax.fori_loop(1, group, send_total, 0)
    wait_all(out, group - 1, recv_sems.at[2])
    wait_all(rs_buf, group - 1, send_sems.at[0])
    wait_all(z_buf, n_lon - 1, send_sems.at[1])
    wait_all(out, group - 1, send_sems.at[2])


def share_prior(pieces, sizes):
    n_lon, n_lat, n_lev = sizes
    group, rows, lanes = pieces.shape
    return pl.pallas_call(
        functools.partial(share_kernel, n_lon, n_lat, n_lev),
        out_shape=jax.ShapeDtypeStruct(pieces.shape, jnp.float32),
        in_specs=[pl.BlockSpec(memory_space=pltpu.VMEM)],
        out_specs=pl.BlockSpec(memory_space=pltpu.VMEM),
        scratch_shapes=[
            pltpu.VMEM((group, rows, lanes), jnp.float32),
            pltpu.VMEM((n_lon, rows, lanes), jnp.float32),
            pltpu.SemaphoreType.DMA((3,)),
            pltpu.SemaphoreType.DMA((3,)),
        ],
        compiler_params=pltpu.CompilerParams(
            has_side_effects=True, vmem_limit_bytes=16 * 1024 * 1024
        ),
        name="share_prior",
    )(pieces)


def split(x):
    hi = x.astype(jnp.bfloat16)
    lo = (x - hi.astype(jnp.float32)).astype(jnp.bfloat16)
    return hi, lo


def taper_of(r2):
    inv = lax.rsqrt(jnp.maximum(r2, 1e-30))
    r = r2 * inv
    inner = 1.0 + r2 * (-5.0 / 3.0 + r * (0.625 + r * (0.5 - 0.25 * r)))
    outer = (
        4.0
        - (2.0 / 3.0) * inv
        + r * (-5.0 + r * (5.0 / 3.0 + r * (0.625 + r * (-0.5 + r * (1.0 / 12.0)))))
    )
    return jnp.where(r2 <= 1.0, inner, jnp.where(r2 < 4.0, outer, 0.0))


def dot(a, b):
    return jnp.dot(a, b, preferred_element_type=jnp.float32)


def innovation(prior, value, err):
    members = prior.shape[0]
    centre = jnp.sum(prior, axis=0, keepdims=True) * (1.0 / members)
    spread = prior - centre
    variance = jnp.sum(spread * spread, axis=0, keepdims=True) * (1.0 / (members - 1))
    denominator = variance + err
    factor = 1.0 / (1.0 + jnp.sqrt(err / denominator))
    gain = (value - centre - factor * spread) / denominator
    return spread, gain


def spread_operand(spread):
    members, count = spread.shape
    hi, lo = split(spread * (1.0 / (members - 1)))
    pad = jnp.zeros((256 - 3 * members, count), jnp.float32)
    stacked = jnp.concatenate(
        [hi.astype(jnp.float32), lo.astype(jnp.float32), hi.astype(jnp.float32), pad], axis=0
    )
    return stacked.T.astype(jnp.bfloat16)


def anomaly_operand(x):
    members = x.shape[0]
    a = x - jnp.sum(x, axis=0, keepdims=True) * (1.0 / members)
    hi, lo = split(a)
    pad = jnp.zeros((256 - 3 * members, x.shape[1]), jnp.bfloat16)
    return jnp.concatenate([hi, hi, lo, pad], axis=0)


def apply_gain(gain_stack, gain_hi, weighted):
    members = gain_hi.shape[0]
    hi, lo = split(weighted)
    both = dot(gain_stack, hi)
    return both[:members] + both[members:] + dot(gain_hi, lo)


def assimilate_kernel(
    lat_rows, members, fields,
    x_ref, prior_ref, value_ref, err_ref, rowk_ref, colk_ref, rowl_ref, coll_ref, out_ref,
    s_op, g_op, lon_part, row_part,
):
    cols = x_ref.shape[-1]
    lat0 = lax.axis_index("lat") * lat_rows
    lon0 = lax.axis_index("lon") * cols
    n_total = cols * lax.axis_size("lon")
    batches, _, count = prior_ref.shape

    def lon_sq(gap):
        gap = jnp.abs(gap)
        gap = jnp.minimum(gap, n_total - gap).astype(jnp.float32) * (1.0 / (n_total // 2))
        return gap * gap

    prior = prior_ref[0]
    for b in range(batches):
        spread, gain = innovation(prior, value_ref[b : b + 1], err_ref[b : b + 1])
        s_op[b] = spread_operand(spread)
        ghi, glo = split(gain)
        g_op[b] = jnp.concatenate([ghi, glo], axis=0)
        grid_cols = lon0 + lax.broadcasted_iota(jnp.int32, (count, cols), 1)
        lon_part[b] = lon_sq(grid_cols - colk_ref[b])
        row_part[b] = jnp.broadcast_to(rowk_ref[b].astype(jnp.float32), (count, cols))
        if b + 1 < batches:
            prior = prior_ref[b + 1]
            dlat = (rowl_ref[b + 1 : b + 2] - rowk_ref[b]).astype(jnp.float32) * (1.0 / 32.0)
            taper = taper_of(dlat * dlat + lon_sq(coll_ref[b + 1 : b + 2] - colk_ref[b]))
            cov = dot(s_op[b], anomaly_operand(prior))
            prior = prior + apply_gain(g_op[b], ghi, taper * cov)

    def row_step(i, carry):
        x = [x_ref[i, f] for f in range(fields)]
        lat = (lat0 + i).astype(jnp.float32)
        for b in range(batches):
            dlat = (lat - row_part[b]) * (1.0 / 32.0)
            taper = taper_of(dlat * dlat + lon_part[b])
            operand = jnp.concatenate([anomaly_operand(v) for v in x], axis=1)
            cov = dot(s_op[b], operand)
            weighted = jnp.concatenate(
                [taper * cov[:, f * cols : (f + 1) * cols] for f in range(fields)], axis=1
            )
            change = apply_gain(g_op[b], g_op[b, :members], weighted)
            x = [x[f] + change[:, f * cols : (f + 1) * cols] for f in range(fields)]
        for f in range(fields):
            out_ref[i, f] = x[f]
        return carry

    lax.fori_loop(0, lat_rows, row_step, 0)


def assimilate(x, prior, obs_value, obs_error, obs_rows, obs_cols):
    lat_rows, fields, members, cols = x.shape
    batches, _, count = prior.shape
    vmem = pl.BlockSpec(memory_space=pltpu.VMEM)
    return pl.pallas_call(
        functools.partial(assimilate_kernel, lat_rows, members, fields),
        out_shape=jax.ShapeDtypeStruct(x.shape, jnp.float32),
        in_specs=[vmem] * 8,
        out_specs=vmem,
        scratch_shapes=[
            pltpu.VMEM((batches, count, 256), jnp.bfloat16),
            pltpu.VMEM((batches, 2 * members, count), jnp.bfloat16),
            pltpu.VMEM((batches, count, cols), jnp.float32),
            pltpu.VMEM((batches, count, cols), jnp.float32),
        ],
        compiler_params=pltpu.CompilerParams(vmem_limit_bytes=VMEM_LIMIT),
        name="assimilate",
    )(
        x, prior, obs_value, obs_error,
        obs_rows[:, :, None], obs_cols[:, :, None], obs_rows, obs_cols,
    )


WIDTH = 3
SUB = 8


def advect_kernel(
    n_lon, n_lat,
    x_ref, cour_ref, out_ref,
    state, packed, left_in, right_in, fix, coef, edge_coef,
    lat_send, lat_recv, lon_send, lon_recv,
):
    rows, count, cols = x_ref.shape
    lon = lax.axis_index("lon")
    lat = lax.axis_index("lat")
    lev = lax.axis_index("lev")
    has_up = lat > 0
    has_down = lat < n_lat - 1
    east = lax.rem(lon + 1, n_lon)
    west = lax.rem(lon + n_lon - 1, n_lon)
    lane = lax.broadcasted_iota(jnp.int32, (SUB, cols), 1)
    groups = count // SUB
    slot = 2 * WIDTH
    edge_lane = (lane < WIDTH) | (lane >= cols - WIDTH)
    from_left = lax.rem(lane, slot) < WIDTH

    def lat_copy(section, down):
        src = rows if down else WIDTH
        dst = 0 if down else WIDTH + rows
        return pltpu.make_async_remote_copy(
            src_ref=state.at[section, pl.ds(src, WIDTH)],
            dst_ref=state.at[section, pl.ds(dst, WIDTH)],
            send_sem=lat_send.at[section, int(down)],
            recv_sem=lat_recv.at[section, int(down)],
            device_id=(lon, lat + 1 if down else lat - 1, lev),
            device_id_type=MESH,
        )

    def lon_copy(section, to_east):
        return pltpu.make_async_remote_copy(
            src_ref=packed.at[section],
            dst_ref=(left_in if to_east else right_in).at[section],
            send_sem=lon_send.at[section, int(to_east)],
            recv_sem=lon_recv.at[section, int(to_east)],
            device_id=(east if to_east else west, lat, lev),
            device_id_type=MESH,
        )

    state[0, WIDTH : WIDTH + rows] = x_ref[...]

    @pl.when(has_up)
    def _():
        lat_copy(0, False).start()

    @pl.when(has_down)
    def _():
        lat_copy(0, True).start()

    @pl.when(jnp.logical_not(has_up))
    def _():
        for s in range(3):
            state[s, 0:WIDTH] = jnp.zeros((WIDTH, count, cols), jnp.float32)

    @pl.when(jnp.logical_not(has_down))
    def _():
        for s in range(3):
            state[s, rows + WIDTH :] = jnp.zeros((WIDTH, count, cols), jnp.float32)

    def pack(section):
        def step(g, carry):
            sl = pl.ds(pl.multiple_of(g * SUB, SUB), SUB)
            acc = jnp.zeros((SUB, cols), jnp.float32)
            for r in range(rows):
                rolled = pltpu.roll(state[section, WIDTH + r, sl], WIDTH + slot * r, 1)
                keep = (lane >= slot * r) & (lane < slot * (r + 1))
                acc = jnp.where(keep, rolled, acc)
            packed[section, sl] = acc
            return carry

        lax.fori_loop(0, groups, step, 0, unroll=5)

    for r in range(rows):
        centre = None
        for d in range(2):
            c = jnp.broadcast_to(cour_ref[d, r : r + 1], (SUB, cols))
            up = jnp.maximum(c, 0.0) * (-1.0 / 60.0)
            dn = jnp.minimum(c, 0.0) * (-1.0 / 60.0)
            for o in range(7):
                w = PLUS_WEIGHTS[o] * up if o < 6 else jnp.zeros_like(c)
                if o > 0:
                    w = w + MINUS_WEIGHTS[o - 1] * dn
                if o == 3:
                    centre = w if d == 0 else centre + w
                else:
                    coef[r, d * 7 + o] = w
        coef[r, 3] = centre
    for o in (1, 2, 3):
        left = jnp.zeros((SUB, cols), jnp.float32)
        right = jnp.zeros((SUB, cols), jnp.float32)
        for r in range(rows):
            mid = slot * r + WIDTH
            left = jnp.where(
                (lane >= mid) & (lane < mid + o), pltpu.roll(coef[r, 3 - o], mid, 1), left
            )
            right = jnp.where(
                (lane >= mid - o) & (lane < mid), pltpu.roll(coef[r, 3 + o], mid, 1), right
            )
        edge_coef[0, o - 1] = left
        edge_coef[1, o - 1] = right

    for section in range(3):
        scale = (1.0 / 3.0, 0.5, 1.0)[section]
        pack(section)
        lon_copy(section, True).start()
        lon_copy(section, False).start()
        lon_copy(section, True).wait_recv()
        lon_copy(section, False).wait_recv()

        def fix_step(g, carry):
            sl = pl.ds(pl.multiple_of(g * SUB, SUB), SUB)
            d = jnp.where(from_left, left_in[section, sl], right_in[section, sl])
            d = d - packed[section, sl]
            t = edge_coef[0, 0] * pltpu.roll(d, 1, 1) + edge_coef[1, 0] * pltpu.roll(d, cols - 1, 1)
            for o in (2, 3):
                t = t + edge_coef[0, o - 1] * pltpu.roll(d, o, 1)
                t = t + edge_coef[1, o - 1] * pltpu.roll(d, cols - o, 1)
            fix[sl] = t
            return carry

        lax.fori_loop(0, groups, fix_step, 0, unroll=5)

        def do_row(r, carry):
            shift = lax.rem(2 * cols - WIDTH - slot * r, cols)
            w = [coef[r, o] if o != 10 else None for o in range(14)]
            for g in range(groups):
                sl = pl.ds(g * SUB, SUB)
                q = state[section, WIDTH + r, sl]
                t = w[3] * q
                u = jnp.where(edge_lane, pltpu.roll(fix[sl], shift, 1), 0.0)
                for o in (1, 2, 3):
                    t = t + w[3 - o] * pltpu.roll(q, o, 1)
                    u = u + w[3 + o] * pltpu.roll(q, cols - o, 1)
                    t = t + w[10 - o] * state[section, WIDTH + r - o, sl]
                    u = u + w[10 + o] * state[section, WIDTH + r + o, sl]
                base = q if section == 0 else state[0, WIDTH + r, sl]
                value = base + (t + u) * scale if section < 2 else base + (t + u)
                if section < 2:
                    state[section + 1, WIDTH + r, sl] = value
                else:
                    out_ref[r, sl] = value
            return carry

        lax.fori_loop(WIDTH, rows - WIDTH, do_row, 0)

        @pl.when(has_up)
        def _():
            lat_copy(section, True).wait_recv()

        @pl.when(has_down)
        def _():
            lat_copy(section, False).wait_recv()

        lax.fori_loop(0, WIDTH, do_row, 0)
        if section < 2:

            @pl.when(has_up)
            def _():
                lat_copy(section + 1, False).start()

        lax.fori_loop(rows - WIDTH, rows, do_row, 0)
        if section < 2:

            @pl.when(has_down)
            def _():
                lat_copy(section + 1, True).start()

    for section in range(3):
        lon_copy(section, True).wait_send()
        lon_copy(section, False).wait_send()

        @pl.when(has_up)
        def _():
            lat_copy(section, False).wait_send()

        @pl.when(has_down)
        def _():
            lat_copy(section, True).wait_send()


def advect(x, courant, sizes):
    n_lon, n_lat, _ = sizes
    rows, count, cols = x.shape
    vmem = pl.BlockSpec(memory_space=pltpu.VMEM)
    return pl.pallas_call(
        functools.partial(advect_kernel, n_lon, n_lat),
        out_shape=jax.ShapeDtypeStruct(x.shape, jnp.float32),
        in_specs=[vmem] * 2,
        out_specs=vmem,
        scratch_shapes=[
            pltpu.VMEM((3, rows + 2 * WIDTH, count, cols), jnp.float32),
            pltpu.VMEM((3, count, cols), jnp.float32),
            pltpu.VMEM((3, count, cols), jnp.float32),
            pltpu.VMEM((3, count, cols), jnp.float32),
            pltpu.VMEM((count, cols), jnp.float32),
            pltpu.VMEM((rows, 14, SUB, cols), jnp.float32),
            pltpu.VMEM((2, WIDTH, SUB, cols), jnp.float32),
            pltpu.SemaphoreType.DMA((3, 2)),
            pltpu.SemaphoreType.DMA((3, 2)),
            pltpu.SemaphoreType.DMA((3, 2)),
            pltpu.SemaphoreType.DMA((3, 2)),
        ],
        compiler_params=pltpu.CompilerParams(has_side_effects=True, vmem_limit_bytes=VMEM_LIMIT),
        name="advect",
    )(x, courant)


def on_device(ensemble, courant, obs_value, obs_error, owner_device, columns):
    members, fields, _, lat_rows, cols = ensemble.shape
    sizes = tuple(lax.axis_size(a) for a in ("lon", "lat", "lev"))
    n_lon, n_lat, n_lev = sizes
    batches, count = columns.shape
    lon_index = owner_device // (n_lat * n_lev)
    lat_index = owner_device // n_lev % n_lat
    obs_rows = lat_index[:, None] * lat_rows + columns // cols
    obs_cols = lon_index[:, None] * cols + columns % cols
    me = (lax.axis_index("lon") * n_lat + lax.axis_index("lat")) * n_lev + lax.axis_index("lev")

    first = ensemble[:, 0, 0].reshape(members, lat_rows * cols)
    cand = jnp.take(first, columns.reshape(-1), axis=1).reshape(members, batches, count)
    cand = jnp.where((owner_device == me)[None, :, None], cand, 0.0)
    group = n_lat * n_lev
    pieces = cand.reshape(group, members * batches * count // (group * 128), 128)
    prior = share_prior(pieces, sizes).reshape(members, batches, count).transpose(1, 0, 2)

    x = ensemble[:, :, 0].transpose(2, 1, 0, 3)
    x = assimilate(x, prior, obs_value, obs_error, obs_rows, obs_cols)
    x = x.reshape(lat_rows, fields * members, cols)
    x = advect(x, courant[:, 0], sizes)
    x = x.reshape(lat_rows, fields, members, cols).transpose(2, 1, 0, 3)
    return x[:, :, None]


def solution(mesh):
    return jax.shard_map(
        on_device,
        mesh=mesh,
        in_specs=(
            P(None, None, "lev", "lat", "lon"),
            P(None, "lev", "lat", "lon"),
            P(),
            P(),
            P(),
            P(),
        ),
        out_specs=P(None, None, "lev", "lat", "lon"),
        check_vma=False,
    )
```

time: 722 us -> 113 us (0.16); the launches traced: 713 us -> 113 us
  waiting for transfers between devices: 448 us -> 0 us
  Pallas kernels: 0 us -> 99.6 us
  local copies, waits for them, and re-layouts: 103 us -> 10.5 us
  other arithmetic: 72.7 us -> 2.91 us
  matrix products: 37.8 us -> 0 us
  starting transfers between devices: 32.1 us -> 0 us
  between operations: 20.4 us -> 0.11 us
    psum x2 -> x0, waiting for transfers between devices: 448 us -> none  [from_root(): return lax.psum(block, axis)]
    pallas_call x0 -> x3, Pallas kernels: none -> 99.6 us  [the longest x1 48 us: advect(): pl.pallas_call(functools.partial(advect_kernel, n_lon, n_lat), out_shape=...]
    add x5 -> x1, other arithmetic: 56.6 us -> 0.75 us  [on_device(): obs_cols = lon_index[:, None] * cols + columns % cols]
    dot_general x4 -> x0, matrix products: 37.8 us -> none  [the longest x2 19 us: regress_all(): jnp.dot(obs_spread.T, anomaly.reshape(members, field_count * cell_count),...]
    ppermute x12 -> x0, starting transfers between devices: 32.1 us -> none  [the longest x6 26 us: padded_2(): after = lax.ppermute(initial, axis, down)]
    slice x14 -> x3, local copies, waits for them, and re-layouts: 27.4 us -> 0.36 us  [on_device(): first = ensemble[:, 0, 0].reshape(members, lat_rows * cols)]
    mul x4 -> x0, local copies, waits for them, and re-layouts: 22.6 us -> none  [regress_all(): weights[:, None, :] * covariance.reshape(-1, field_count, cell_count)]
    ppermute x6 -> x0, local copies, waits for them, and re-layouts: 18.4 us -> none  [the longest x3 9.19 us: padded_2(): after = lax.ppermute(initial, axis, down)]
  transfers between devices with their start and end apart: 14 -> 0, of which waited for: 2 -> 0; matrix products, arithmetic and copies ran while one was open for 11% -> 0% of each run, Pallas kernels for 0% -> 0%
where the time goes in v1:
time: 113 us
  Pallas kernels  99.6 us (88%)
  local copies, waits for them, and re-layouts  10.5 us (9%)
  other arithmetic  2.91 us (3%)
    pallas_call x1, Pallas kernels, advect(): pl.pallas_call(functools.partial(advect_kernel, n_lon, n_lat), out_shape=...  48 us
    pallas_call x1, Pallas kernels, share_prior(): pl.pallas_call(functools.partial(share_kernel, n_lon, n_lat, n_lev), out_...  31.8 us
    pallas_call x1, Pallas kernels, assimilate(): pl.pallas_call(functools.partial(assimilate_kernel, lat_rows, members, fi...  19.7 us
    reshape x1, local copies, waits for them, and re-layouts, on_device(): x = x.reshape(lat_rows, fields, members, cols).transpose(2, 1, 0, 3)  3.45 us
    unnamed x8, local copies, waits for them, and re-layouts  2.57 us

profile of v1, /device:TPU:8, one launch (start us, length us, event | category | flops | bytes accessed | tf_op | source)
XLA Modules:
  0.0 113.1 jit_solution(832013480066241838)
XLA Ops:
  0.0 0.7 broadcast_compare_fusion.2
  0.7 0.7 compare_and_fusion
  1.4 0.7 fusion.4
  2.1 0.7 copy.20
  2.8 0.8 fusion
  3.6 0.1 broadcast_in_dim.41
  3.7 0.1 broadcast_in_dim.38
  3.8 0.1 broadcast_in_dim.39
  4.0 0.9 copy.17.rowk_ref
  4.8 0.9 copy.18.colk_ref
  5.7 0.4 copy.14
  6.1 0.0 copy-done.1
  6.1 0.0 copy-done.2
  6.1 0.0 copy-start
  6.1 1.0 gather_fusion
  7.1 0.1 copy.15
  7.3 0.1 select_select_fusion.cand
  7.4 31.8 %share_prior.1 = f32[32,10,128]{2,1,0:T(8,128)S(1)} custom-call(f32[32,10,128]{2,1,0:T(8,128)S(1)} %select_select_fusion.cand), custom_call_target="tpu_custom_call" | custom-call | tf_op jit(solution)/shard_map/share_prior/pallas_call | solution.py:82
  39.2 0.1 reshape.62
  39.3 0.7 copy.26
  40.0 1.9 %copy.25 = f32[80,3,1,16,128]{4,0,1,3,2:T(8,128)} copy(f32[80,3,1,16,128]{4,3,2,1,0:T(8,128)S(1)} %copy-done) | data formatting | bytes 3932160 | tf_op args[0]
  41.9 19.7 %assimilate.1 = f32[16,3,80,128]{3,2,1,0:T(8,128)} custom-call(f32[16,3,80,128]{3,2,1,0:T(8,128)} %bitcast.28, f32[2,80,256]{2,1,0:T(8,128)} %bitcast.32, f32[2,256]{1,0:T(2,128)} %value_ref.1, f32[2,256]{1,0:T(2,128)} %err_ref.1, s32[2,256,1]{2,1,0:T(8,128)} %copy.17.rowk_ref, s32[2,256,1]{2,1,0:T(8,128)} %copy.18.colk_ref, s32[2,256]{1,0:T(2,128)} %copy-done.2, ...), custom_call_target="tpu_custom_call" | custom-call | tf_op jit(solution)/shard_map/assimilate/pallas_call | solution.py:214
  61.6 48.0 %advect.1 = f32[16,240,128]{2,1,0:T(8,128)} custom-call(f32[16,240,128]{2,1,0:T(8,128)} %bitcast.27, f32[2,16,128]{2,1,0:T(8,128)} %bitcast.36), custom_call_target="tpu_custom_call" | custom-call | tf_op jit(solution)/shard_map/advect/pallas_call | solution.py:424
  109.6 3.5 %copy.24 = f32[16,3,80,128]{3,0,1,2:T(8,128)} copy(f32[16,3,80,128]{3,2,1,0:T(8,128)} %bitcast.29) | data formatting | bytes 3932160 | tf_op jit(solution)/shard_map/reshape | solution.py:469
  (9 shorter events, 0.1 us)
Async XLA Ops:
  0.0 5.7 %slice-start = ((f32[80,3,1,16,128]{4,3,2,1,0:T(8,128)}), f32[80,1,1,16,128]{4,3,2,1,0:T(8,128)S(1)}, s32[]{:S(2)}) async-start(f32[80,3,1,16,128]{4,3,2,1,0:T(8,128)} %param.6), calls=%async_computation | async-start | bytes 1310720 | tf_op jit(solution)/shard_map/slice | solution.py:458
  3.5 2.5 %copy-start.1 = (s32[2,256]{1,0:T(2,128)}, s32[2,256]{1,0:T(2,128)S(1)}, u32[]{:S(2)}) copy-start(s32[2,256]{1,0:T(2,128)S(1)} %get-tuple-element.5.coll_ref) | copy-start | bytes 6148
  3.5 2.5 %copy-start.2 = (s32[2,256]{1,0:T(2,128)}, s32[2,256]{1,0:T(2,128)S(1)}, u32[]{:S(2)}) copy-start(s32[2,256]{1,0:T(2,128)S(1)} %get-tuple-element.6.rowl_ref) | copy-start | bytes 6148
  6.1 33.9 %copy-start = (f32[80,3,1,16,128]{4,3,2,1,0:T(8,128)S(1)}, f32[80,3,1,16,128]{4,3,2,1,0:T(8,128)}, u32[]{:S(2)}) copy-start(f32[80,3,1,16,128]{4,3,2,1,0:T(8,128)} %param.6) | copy-start | bytes 5898244

commit v2 on v0

v2 whole, which is shorter than its diff:
```python
import functools

import jax
import jax.numpy as jnp
from jax import lax
from jax.experimental import pallas as pl
from jax.experimental.pallas import tpu as pltpu
from jax.sharding import PartitionSpec as P

MESH = pl.DeviceIdType.MESH
PLUS_WEIGHTS = (-2.0, 15.0, -60.0, 20.0, 30.0, -3.0)
MINUS_WEIGHTS = (3.0, -30.0, -20.0, 60.0, -15.0, 2.0)
VMEM_LIMIT = 60 * 1024 * 1024
WIDTH = 3
SUB = 8
ROWS = 4
LANES = 128


def split(x):
    hi = x.astype(jnp.bfloat16)
    lo = (x - hi.astype(jnp.float32)).astype(jnp.bfloat16)
    return hi, lo


def taper_of(r2):
    inv = lax.rsqrt(jnp.maximum(r2, 1e-30))
    r = r2 * inv
    inner = 1.0 + r2 * (-5.0 / 3.0 + r * (0.625 + r * (0.5 - 0.25 * r)))
    outer = (
        4.0
        - (2.0 / 3.0) * inv
        + r * (-5.0 + r * (5.0 / 3.0 + r * (0.625 + r * (-0.5 + r * (1.0 / 12.0)))))
    )
    return jnp.where(r2 <= 1.0, inner, jnp.where(r2 < 4.0, outer, 0.0))


def dot(a, b):
    return jnp.dot(a, b, preferred_element_type=jnp.float32)


def innovation(prior, value, err):
    members = prior.shape[0]
    centre = jnp.sum(prior, axis=0, keepdims=True) * (1.0 / members)
    spread = prior - centre
    variance = jnp.sum(spread * spread, axis=0, keepdims=True) * (1.0 / (members - 1))
    denominator = variance + err
    factor = 1.0 / (1.0 + jnp.sqrt(err / denominator))
    gain = (value - centre - factor * spread) / denominator
    return spread, gain


def spread_operand(spread):
    members, count = spread.shape
    hi, lo = split(spread * (1.0 / (members - 1)))
    pad = jnp.zeros((256 - 3 * members, count), jnp.float32)
    stacked = jnp.concatenate(
        [hi.astype(jnp.float32), lo.astype(jnp.float32), hi.astype(jnp.float32), pad], axis=0
    )
    return stacked.T.astype(jnp.bfloat16)


def anomaly_operand(x):
    members = x.shape[0]
    a = x - jnp.sum(x, axis=0, keepdims=True) * (1.0 / members)
    hi, lo = split(a)
    pad = jnp.zeros((256 - 3 * members, x.shape[1]), jnp.bfloat16)
    return jnp.concatenate([hi, hi, lo, pad], axis=0)


def apply_gain(gain_stack, gain_hi, weighted):
    members = gain_hi.shape[0]
    hi, lo = split(weighted)
    both = dot(gain_stack, hi)
    return both[:members] + both[members:] + dot(gain_hi, lo)


def kernel(
    dims,
    x_ref, cour_ref, value_ref, err_ref, local_ref, rowk_ref, colk_ref, rowl_ref, coll_ref, out_ref,
    cand, peer, mine, rs_buf, z_buf, full, prior_buf,
    s_op, g_op, lon_part, row_part, taper_buf,
    state, packed, left_in, right_in, fix, coef, edge_coef,
    share_send, share_recv, lat_send, lat_recv, lon_send, lon_recv,
):
    n_lon, n_lat, n_lev = dims
    rows, fields, members, cols = x_ref.shape
    batches, count = value_ref.shape
    total = fields * members
    lon = lax.axis_index("lon")
    lat = lax.axis_index("lat")
    lev = lax.axis_index("lev")
    has_up = lat > 0
    has_down = lat < n_lat - 1
    east = lax.rem(lon + 1, n_lon)
    west = lax.rem(lon + n_lon - 1, n_lon)
    other_lev = 1 - lev
    slot = 2 * WIDTH
    per = members // n_lat

    barrier = pltpu.get_barrier_semaphore()

    def greet_lat(t, carry):
        pl.semaphore_signal(
            barrier, inc=1, device_id=(lon, lax.rem(lat + t, n_lat), lev), device_id_type=MESH
        )
        return carry

    def greet_lon(t, carry):
        pl.semaphore_signal(
            barrier, inc=1, device_id=(lax.rem(lon + t, n_lon), lat, lev), device_id_type=MESH
        )
        return carry

    pl.semaphore_signal(barrier, inc=1, device_id=(lon, lat, other_lev), device_id_type=MESH)
    lax.fori_loop(1, n_lat, greet_lat, 0)
    lax.fori_loop(1, n_lon, greet_lon, 0)

    picked = None
    for pair in range(rows // 2):
        parts = [x_ref[2 * pair + j, 0] for j in range(2)]
        x0 = jnp.concatenate(parts, axis=1)
        hi = x0.astype(jnp.bfloat16)
        rest = x0 - hi.astype(jnp.float32)
        mid, lo = split(rest)
        cell = lax.broadcasted_iota(jnp.int32, (2 * cols, count), 0) + pair * 2 * cols
        hot = [
            jnp.where(cell == local_ref[b : b + 1], 1.0, 0.0).astype(jnp.bfloat16)
            for b in range(batches)
        ]
        term = dot(jnp.concatenate([hi, mid, lo], axis=0), jnp.concatenate(hot, axis=1))
        picked = term if picked is None else picked + term
    picked = picked[:members] + (picked[members : 2 * members] + picked[2 * members :])
    halves = count // LANES
    for b in range(batches):
        for p in range(n_lat):
            for h in range(halves):
                at = b * count + h * LANES
                cand[b, p, h * per : (h + 1) * per] = picked[p * per : (p + 1) * per, at : at + LANES]

    pl.semaphore_wait(barrier, n_lat + n_lon - 1)

    def wait_all(buf, number, sem):
        view = buf.at[pl.ds(0, number)]
        pltpu.make_async_copy(view, view, sem).wait()

    def swap_cand():
        return pltpu.make_async_remote_copy(
            src_ref=cand.at[other_lev], dst_ref=peer,
            send_sem=share_send.at[0], recv_sem=share_recv.at[0],
            device_id=(lon, lat, other_lev), device_id_type=MESH,
        )

    def send_piece(t, carry):
        other = lax.rem(lat + t, n_lat)
        pltpu.make_async_remote_copy(
            src_ref=mine.at[other], dst_ref=rs_buf.at[lat],
            send_sem=share_send.at[1], recv_sem=share_recv.at[1],
            device_id=(lon, other, lev), device_id_type=MESH,
        ).start()
        return carry

    def send_sum(t, carry):
        pltpu.make_async_remote_copy(
            src_ref=z_buf.at[lon], dst_ref=z_buf.at[lon],
            send_sem=share_send.at[2], recv_sem=share_recv.at[2],
            device_id=(lax.rem(lon + t, n_lon), lat, lev), device_id_type=MESH,
        ).start()
        return carry

    def send_total(t, carry):
        pltpu.make_async_remote_copy(
            src_ref=full.at[lev, lat], dst_ref=full.at[lev, lat],
            send_sem=share_send.at[3], recv_sem=share_recv.at[3],
            device_id=(lon, lax.rem(lat + t, n_lat), lev), device_id_type=MESH,
        ).start()
        return carry

    def swap_full():
        return pltpu.make_async_remote_copy(
            src_ref=full.at[lev], dst_ref=full.at[lev],
            send_sem=share_send.at[4], recv_sem=share_recv.at[4],
            device_id=(lon, lat, other_lev), device_id_type=MESH,
        )

    lat0 = lat * rows
    lon0 = lon * cols
    n_total = cols * n_lon

    def lon_sq(gap):
        gap = jnp.abs(gap)
        gap = jnp.minimum(gap, n_total - gap).astype(jnp.float32) * (1.0 / (n_total // 2))
        return gap * gap

    def tapers(first, last):
        def one(n, carry):
            b = n // rows
            i = lax.rem(n, rows)
            here = (lat0 + i).astype(jnp.float32)
            for at in range(0, count, 64):
                sl = pl.ds(at, 64)
                dlat = (here - row_part[b, sl]) * (1.0 / (2.0 * rows))
                taper_buf[b, i, sl] = taper_of(dlat * dlat + lon_part[b, sl])
            return carry

        lax.fori_loop(first, last, one, 0)

    swap_cand().start()
    for b in range(batches):
        grid_cols = lon0 + lax.broadcasted_iota(jnp.int32, (count, cols), 1)
        lon_part[b] = lon_sq(grid_cols - colk_ref[b])
        row_part[b] = jnp.broadcast_to(rowk_ref[b].astype(jnp.float32), (count, cols))
    swap_cand().wait_recv()
    for p in range(n_lat):
        mine[p] = cand[lev, p] + peer[p]
    lax.fori_loop(1, n_lat, send_piece, 0)
    rs_buf[lat] = mine[lat]
    tapers(0, 12)
    wait_all(rs_buf, n_lat - 1, share_recv.at[1])
    z_buf[lon] = jnp.sum(rs_buf[...], axis=0)
    lax.fori_loop(1, n_lon, send_sum, 0)
    tapers(12, 22)
    wait_all(z_buf, n_lon - 1, share_recv.at[2])
    full[lev, lat] = jnp.sum(z_buf[...], axis=0)
    lax.fori_loop(1, n_lat, send_total, 0)
    tapers(22, 2 * rows)
    wait_all(full.at[lev], n_lat - 1, share_recv.at[3])
    swap_full().start()

    lane = lax.broadcasted_iota(jnp.int32, (SUB, cols), 1)
    edge_lane = (lane < WIDTH) | (lane >= cols - WIDTH)
    from_left = lax.rem(lane, slot) < WIDTH
    for r in range(rows):
        centre = None
        for d in range(2):
            c = jnp.broadcast_to(cour_ref[d, r : r + 1], (SUB, cols))
            up = jnp.maximum(c, 0.0) * (-1.0 / 60.0)
            dn = jnp.minimum(c, 0.0) * (-1.0 / 60.0)
            for o in range(7):
                w = PLUS_WEIGHTS[o] * up if o < 6 else jnp.zeros_like(c)
                if o > 0:
                    w = w + MINUS_WEIGHTS[o - 1] * dn
                if o == 3:
                    centre = w if d == 0 else centre + w
                else:
                    coef[r, d * 7 + o] = w
        coef[r, 3] = centre
    for o in (1, 2, 3):
        left = jnp.zeros((SUB, cols), jnp.float32)
        right = jnp.zeros((SUB, cols), jnp.float32)
        for r in range(rows):
            mid = slot * r + WIDTH
            left = jnp.where(
                (lane >= mid) & (lane < mid + o), pltpu.roll(coef[r, 3 - o], mid, 1), left
            )
            right = jnp.where(
                (lane >= mid - o) & (lane < mid), pltpu.roll(coef[r, 3 + o], mid, 1), right
            )
        edge_coef[0, o - 1] = left
        edge_coef[1, o - 1] = right

    @pl.when(jnp.logical_not(has_up))
    def _():
        for s in range(3):
            state[s, 0:WIDTH] = jnp.zeros((WIDTH, total, cols), jnp.float32)

    @pl.when(jnp.logical_not(has_down))
    def _():
        for s in range(3):
            state[s, rows + WIDTH :] = jnp.zeros((WIDTH, total, cols), jnp.float32)

    swap_full().wait_recv()
    for b in range(batches):
        for p in range(n_lat):
            for h in range(halves):
                at = h * LANES
                prior_buf[b, p * per : (p + 1) * per, at : at + LANES] = full[
                    b, p, h * per : (h + 1) * per
                ]

    prior = prior_buf[0]
    for b in range(batches):
        spread, gain = innovation(prior, value_ref[b : b + 1], err_ref[b : b + 1])
        s_op[b] = spread_operand(spread)
        ghi, glo = split(gain)
        g_op[b] = jnp.concatenate([ghi, glo], axis=0)
        if b + 1 < batches:
            prior = prior_buf[b + 1]
            dlat = (rowl_ref[b + 1 : b + 2] - rowk_ref[b]).astype(jnp.float32)
            dlat = dlat * (1.0 / (2.0 * rows))
            taper = taper_of(dlat * dlat + lon_sq(coll_ref[b + 1 : b + 2] - colk_ref[b]))
            cov = dot(s_op[b], anomaly_operand(prior))
            prior = prior + apply_gain(g_op[b], ghi, taper * cov)

    def assimilate(i0):
        every = [(i0 + j, f) for j in range(ROWS) for f in range(fields)]
        x = [x_ref[i, f] for i, f in every]
        for b in range(batches):
            operand = jnp.concatenate([anomaly_operand(v) for v in x], axis=1)
            cov = dot(s_op[b], operand)
            weighted = jnp.concatenate(
                [
                    taper_buf[b, i] * cov[:, n * cols : (n + 1) * cols]
                    for n, (i, _) in enumerate(every)
                ],
                axis=1,
            )
            change = apply_gain(g_op[b], g_op[b, :members], weighted)
            x = [v + change[:, n * cols : (n + 1) * cols] for n, v in enumerate(x)]
        for (i, f), v in zip(every, x):
            state[0, WIDTH + i, f * members : (f + 1) * members] = v

    def field_slice(c):
        return pl.ds(c * members, members)

    def lat_copy(section, c, down):
        src = rows if down else WIDTH
        dst = 0 if down else WIDTH + rows
        return pltpu.make_async_remote_copy(
            src_ref=state.at[section, pl.ds(src, WIDTH), field_slice(c)],
            dst_ref=state.at[section, pl.ds(dst, WIDTH), field_slice(c)],
            send_sem=lat_send.at[section, c, int(down)],
            recv_sem=lat_recv.at[section, c, int(down)],
            device_id=(lon, lat + 1 if down else lat - 1, lev),
            device_id_type=MESH,
        )

    def lat_start(section, c):
        @pl.when(has_up)
        def _():
            lat_copy(section, c, False).start()

        @pl.when(has_down)
        def _():
            lat_copy(section, c, True).start()

    def lon_copy(section, c, to_east):
        return pltpu.make_async_remote_copy(
            src_ref=packed.at[section, field_slice(c)],
            dst_ref=(left_in if to_east else right_in).at[section, field_slice(c)],
            send_sem=lon_send.at[section, c, int(to_east)],
            recv_sem=lon_recv.at[section, c, int(to_east)],
            device_id=(east if to_east else west, lat, lev),
            device_id_type=MESH,
        )

    per_field = members // SUB

    def lon_start(section, c):
        def step(g, carry):
            sl = pl.ds(pl.multiple_of(c * members + g * SUB, SUB), SUB)
            acc = jnp.zeros((SUB, cols), jnp.float32)
            for r in range(rows):
                rolled = pltpu.roll(state[section, WIDTH + r, sl], WIDTH + slot * r, 1)
                keep = (lane >= slot * r) & (lane < slot * (r + 1))
                acc = jnp.where(keep, rolled, acc)
            packed[section, sl] = acc
            return carry

        lax.fori_loop(0, per_field, step, 0, unroll=5)
        lon_copy(section, c, True).start()
        lon_copy(section, c, False).start()

    last = rows - ROWS
    lax.fori_loop(0, 2, lambda n, carry: (assimilate(n * last), carry)[1], 0)
    for c in range(fields):
        lat_start(0, c)
    lax.fori_loop(1, last // ROWS, lambda n, carry: (assimilate(n * ROWS), carry)[1], 0)

    def do_rows(section, c, first, stop):
        scale = (1.0 / 3.0, 0.5, 1.0)[section]

        def do_row(r, carry):
            shift = lax.rem(2 * cols - WIDTH - slot * r, cols)
            w = [coef[r, o] if o != 10 else None for o in range(14)]
            for g in range(per_field):
                sl = pl.ds(c * members + g * SUB, SUB)
                q = state[section, WIDTH + r, sl]
                t = w[3] * q
                u = jnp.where(edge_lane, pltpu.roll(fix[sl], shift, 1), 0.0)
                for o in (1, 2, 3):
                    t = t + w[3 - o] * pltpu.roll(q, o, 1)
                    u = u + w[3 + o] * pltpu.roll(q, cols - o, 1)
                    t = t + w[10 - o] * state[section, WIDTH + r - o, sl]
                    u = u + w[10 + o] * state[section, WIDTH + r + o, sl]
                base = q if section == 0 else state[0, WIDTH + r, sl]
                if section < 2:
                    state[section + 1, WIDTH + r, sl] = base + (t + u) * scale
                else:
                    at = (g * SUB * fields + c) * rows + r
                    out_ref[pl.ds(at, SUB, stride=fields * rows), :] = base + (t + u)
            return carry

        lax.fori_loop(first, stop, do_row, 0)

    for c in range(fields):
        lon_start(0, c)

    for section in range(3):
        for c in range(fields):
            lon_copy(section, c, True).wait_recv()
            lon_copy(section, c, False).wait_recv()

            def fix_step(g, carry):
                sl = pl.ds(pl.multiple_of(c * members + g * SUB, SUB), SUB)
                d = jnp.where(from_left, left_in[section, sl], right_in[section, sl])
                d = d - packed[section, sl]
                t = jnp.zeros((SUB, cols), jnp.float32)
                for o in (1, 2, 3):
                    t = t + edge_coef[0, o - 1] * pltpu.roll(d, o, 1)
                    t = t + edge_coef[1, o - 1] * pltpu.roll(d, cols - o, 1)
                fix[sl] = t
                return carry

            lax.fori_loop(0, per_field, fix_step, 0, unroll=5)
            do_rows(section, c, WIDTH, rows - WIDTH)

            @pl.when(has_up)
            def _():
                lat_copy(section, c, True).wait_recv()

            @pl.when(has_down)
            def _():
                lat_copy(section, c, False).wait_recv()

            do_rows(section, c, 0, WIDTH)
            do_rows(section, c, rows - WIDTH, rows)
            if section < 2:
                lat_start(section + 1, c)
                lon_start(section + 1, c)

    swap_cand().wait_send()
    wait_all(rs_buf, n_lat - 1, share_send.at[1])
    wait_all(z_buf, n_lon - 1, share_send.at[2])
    wait_all(full.at[lev], n_lat - 1, share_send.at[3])
    swap_full().wait_send()
    for section in range(3):
        for c in range(fields):
            lon_copy(section, c, True).wait_send()
            lon_copy(section, c, False).wait_send()

            @pl.when(has_up)
            def _():
                lat_copy(section, c, False).wait_send()

            @pl.when(has_down)
            def _():
                lat_copy(section, c, True).wait_send()


def on_device(ensemble, courant, obs_value, obs_error, owner_device, columns):
    members, fields, _, rows, cols = ensemble.shape
    dims = tuple(lax.axis_size(a) for a in ("lon", "lat", "lev"))
    n_lon, n_lat, n_lev = dims
    batches, count = columns.shape
    lon_index = owner_device // (n_lat * n_lev)
    lat_index = owner_device // n_lev % n_lat
    obs_rows = lat_index[:, None] * rows + columns // cols
    obs_cols = lon_index[:, None] * cols + columns % cols
    me = (lax.axis_index("lon") * n_lat + lax.axis_index("lat")) * n_lev + lax.axis_index("lev")
    local = jnp.where((owner_device == me)[:, None], columns, -1)

    x = ensemble[:, :, 0].transpose(2, 1, 0, 3)
    total = fields * members
    piece = (members // n_lat * count // LANES, LANES)
    f32, bf16 = jnp.float32, jnp.bfloat16
    vmem = pl.BlockSpec(memory_space=pltpu.VMEM)
    dma = pltpu.SemaphoreType.DMA
    out = pl.pallas_call(
        functools.partial(kernel, dims),
        out_shape=jax.ShapeDtypeStruct((members * fields * rows, cols), f32),
        in_specs=[vmem] * 9,
        out_specs=vmem,
        scratch_shapes=[
            pltpu.VMEM((batches, n_lat) + piece, f32),
            pltpu.VMEM((n_lat,) + piece, f32),
            pltpu.VMEM((n_lat,) + piece, f32),
            pltpu.VMEM((n_lat,) + piece, f32),
            pltpu.VMEM((n_lon,) + piece, f32),
            pltpu.VMEM((batches, n_lat) + piece, f32),
            pltpu.VMEM((batches, members, count), f32),
            pltpu.VMEM((batches, count, 256), bf16),
            pltpu.VMEM((batches, 2 * members, count), bf16),
            pltpu.VMEM((batches, count, cols), f32),
            pltpu.VMEM((batches, count, cols), f32),
            pltpu.VMEM((batches, rows, count, cols), f32),
            pltpu.VMEM((3, rows + 2 * WIDTH, total, cols), f32),
            pltpu.VMEM((3, total, cols), f32),
            pltpu.VMEM((3, total, cols), f32),
            pltpu.VMEM((3, total, cols), f32),
            pltpu.VMEM((total, cols), f32),
            pltpu.VMEM((rows, 14, SUB, cols), f32),
            pltpu.VMEM((2, WIDTH, SUB, cols), f32),
            dma((5,)),
            dma((5,)),
            dma((3, fields, 2)),
            dma((3, fields, 2)),
            dma((3, fields, 2)),
            dma((3, fields, 2)),
        ],
        compiler_params=pltpu.CompilerParams(
            has_side_effects=True, collective_id=0, vmem_limit_bytes=VMEM_LIMIT
        ),
        name="filter_and_advect",
    )(
        x, courant[:, 0], obs_value, obs_error, local,
        obs_rows[:, :, None], obs_cols[:, :, None], obs_rows, obs_cols,
    )
    return out.reshape(ensemble.shape)


def solution(mesh):
    return jax.shard_map(
        on_device,
        mesh=mesh,
        in_specs=(
            P(None, None, "lev", "lat", "lon"),
            P(None, "lev", "lat", "lon"),
            P(),
            P(),
            P(),
            P(),
        ),
        out_specs=P(None, None, "lev", "lat", "lon"),
        check_vma=False,
    )
```

time: 722 us -> 76.5 us (0.11)
  the two profiles are of different devices: /device:TPU:8 before, /device:TPU:1 now
where the time goes in v2:
time: 76.5 us; the launch traced here: 76.3 us
  Pallas kernels  65.5 us (86%)
  local copies, waits for them, and re-layouts  8.13 us (11%)
  other arithmetic  2.67 us (3%)
    pallas_call x1, Pallas kernels, on_device(): pl.pallas_call(functools.partial(kernel, dims), out_shape=jax.ShapeDtypeS...  65.5 us
    unnamed x6, local copies, waits for them, and re-layouts  6.4 us

profile of v2, /device:TPU:1, one launch (start us, length us, event | category | flops | bytes accessed | tf_op | source)
XLA Modules:
  0.0 76.3 jit_solution(14056362036468614172)
XLA Ops:
  0.0 0.7 broadcast_compare_fusion.2
  0.7 0.7 fusion.4
  1.3 1.3 %fusion = (s32[2,256]{1,0:T(2,128)S(1)}, s32[2,256]{1,0:T(2,128)}, s32[2,256]{1,0:T(2,128)S(1)}) fusion(s32[2]{0:T(128)S(1)} %get-tuple-element.8, s32[2,256]{1,0:T(2,128)} %param.11, pred[2]{0:T(512)(128)(4,1)S(1)} %broadcast_compare_fusion.2, s32[2]{0:T(128)S(1)} %get-tuple-element.9), kind=kLoop, calls=%fused_computation.8 | loop fusion | flops 11264 | bytes 8210 | tf_op jit(solution)/shard_map/add | solution.py:459
  2.7 0.0 copy-start
  2.7 0.0 copy-start.1
  2.7 0.9 %copy.8.rowk_ref = s32[2,256,1]{2,1,0:T(8,128)} copy(s32[2,256,1]{1,0,2:T(2,128)S(1)} %bitcast.14) | data formatting | bytes 4096 | tf_op jit(solution)/shard_map/broadcast_in_dim | solution.py:507
  3.5 0.9 %copy.9.colk_ref = s32[2,256,1]{2,1,0:T(8,128)} copy(s32[2,256,1]{1,0,2:T(2,128)S(1)} %bitcast.13) | data formatting | bytes 4096 | tf_op jit(solution)/shard_map/broadcast_in_dim | solution.py:507
  4.4 3.4 %copy.12 = f32[80,3,1,16,128]{4,0,1,3,2:T(8,128)} copy(f32[80,3,1,16,128]{4,3,2,1,0:T(8,128)} %param.6) | data formatting | bytes 3932160 | tf_op args[0]
  7.8 0.0 copy-done
  7.9 0.0 copy-done.1
  7.9 65.5 %filter_and_advect.1 = f32[3840,128]{1,0:T(8,128)} custom-call(f32[16,3,80,128]{3,2,1,0:T(8,128)} %bitcast.12, f32[2,16,128]{2,1,0:T(8,128)} %bitcast.15, f32[2,256]{1,0:T(2,128)} %value_ref.1, f32[2,256]{1,0:T(2,128)} %err_ref.1, s32[2,256]{1,0:T(2,128)} %get-tuple-element.6.local_ref, s32[2,256,1]{2,1,0:T(8,128)} %copy.8.rowk_ref, ...), custom_call_target="tpu_custom_call" | custom-call | tf_op jit(solution)/shard_map/filter_and_advect/pallas_call | solution.py:469
  73.3 2.9 %copy.14 = f32[80,3,1,16,128]{4,3,2,1,0:T(8,128)} copy(f32[80,3,1,16,128]{4,3,2,1,0:T(8,128)} %bitcast.11) | data formatting | bytes 3932160
Async XLA Ops:
  2.7 5.2 %copy-start = (s32[2,256]{1,0:T(2,128)}, s32[2,256]{1,0:T(2,128)S(1)}, u32[]{:S(2)}) copy-start(s32[2,256]{1,0:T(2,128)S(1)} %get-tuple-element.5.coll_ref) | copy-start | bytes 6148
  2.7 5.2 %copy-start.1 = (s32[2,256]{1,0:T(2,128)}, s32[2,256]{1,0:T(2,128)S(1)}, u32[]{:S(2)}) copy-start(s32[2,256]{1,0:T(2,128)S(1)} %get-tuple-element.7.rowl_ref) | copy-start | bytes 6148

commit v3 on v2

v3 whole, which is shorter than its diff:
```python
import functools

import jax
import jax.numpy as jnp
from jax import lax
from jax.experimental import pallas as pl
from jax.experimental.pallas import tpu as pltpu
from jax.sharding import PartitionSpec as P

MESH = pl.DeviceIdType.MESH
PLUS_WEIGHTS = (-2.0, 15.0, -60.0, 20.0, 30.0, -3.0)
MINUS_WEIGHTS = (3.0, -30.0, -20.0, 60.0, -15.0, 2.0)
VMEM_LIMIT = 60 * 1024 * 1024
WIDTH = 3
SUB = 8
STEP = 11
SUM_SPAN = 16
PACK_SPAN = 16
LANES = 128


def split(x):
    hi = x.astype(jnp.bfloat16)
    lo = (x - hi.astype(jnp.float32)).astype(jnp.bfloat16)
    return hi, lo


def taper_of(r2):
    inv = lax.rsqrt(jnp.maximum(r2, 1e-30))
    r = r2 * inv
    inner = 1.0 + r2 * (-5.0 / 3.0 + r * (0.625 + r * (0.5 - 0.25 * r)))
    outer = (
        4.0
        - (2.0 / 3.0) * inv
        + r * (-5.0 + r * (5.0 / 3.0 + r * (0.625 + r * (-0.5 + r * (1.0 / 12.0)))))
    )
    return jnp.where(r2 <= 1.0, inner, jnp.where(r2 < 4.0, outer, 0.0))


def dot(a, b):
    return jnp.dot(a, b, preferred_element_type=jnp.float32)


def innovation(prior, value, err):
    members = prior.shape[0]
    centre = jnp.sum(prior, axis=0, keepdims=True) * (1.0 / members)
    spread = prior - centre
    variance = jnp.sum(spread * spread, axis=0, keepdims=True) * (1.0 / (members - 1))
    denominator = variance + err
    factor = 1.0 / (1.0 + jnp.sqrt(err / denominator))
    gain = (value - centre - factor * spread) / denominator
    return spread, gain


def spread_operand(spread):
    members, count = spread.shape
    hi, lo = split(spread * (1.0 / (members - 1)))
    pad = jnp.zeros((256 - 3 * members, count), jnp.float32)
    stacked = jnp.concatenate(
        [hi.astype(jnp.float32), lo.astype(jnp.float32), hi.astype(jnp.float32), pad], axis=0
    )
    return stacked.T.astype(jnp.bfloat16)


def anomaly_operand(x):
    members = x.shape[0]
    a = x - jnp.sum(x, axis=0, keepdims=True) * (1.0 / members)
    hi, lo = split(a)
    pad = jnp.zeros((256 - 3 * members, x.shape[1]), jnp.bfloat16)
    return jnp.concatenate([hi, hi, lo, pad], axis=0)


def apply_gain(gain_stack, gain_hi, weighted):
    members = gain_hi.shape[0]
    hi, lo = split(weighted)
    both = dot(gain_stack, hi)
    return both[:members] + both[members:] + dot(gain_hi, lo)


def kernel(
    dims,
    x_ref, cour_ref, value_ref, err_ref, owner_ref, columns_ref, out_ref,
    cand, rs_buf, z_buf, full, prior_buf,
    s_op, g_op, lon_part, row_part, col_part, taper_buf,
    state, packed, left_in, right_in, lhs, dpm, coef, stencil, picker, slot_mask,
    load_sem, share_send, share_recv, lat_send, lat_recv, lon_send, lon_recv,
):
    n_lon, n_lat, n_lev = dims
    members, fields, _, rows, cols = x_ref.shape
    batches, count = value_ref.shape
    total = fields * members
    lon = lax.axis_index("lon")
    lat = lax.axis_index("lat")
    lev = lax.axis_index("lev")
    has_up = lat > 0
    has_down = lat < n_lat - 1
    east = lax.rem(lon + 1, n_lon)
    west = lax.rem(lon + n_lon - 1, n_lon)
    other_lev = 1 - lev
    slot = 2 * WIDTH
    per = members // n_lat

    def load_start(f):
        def one(i, carry):
            pltpu.make_async_copy(
                x_ref.at[:, f, 0, i],
                state.at[0, WIDTH + i, pl.ds(f * members, members)],
                load_sem.at[f],
            ).start()
            return carry

        lax.fori_loop(0, rows, one, 0)

    def load_wait(f):
        view = state.at[0, pl.ds(WIDTH, rows), pl.ds(f * members, members)]
        pltpu.make_async_copy(view, view, load_sem.at[f]).wait()

    for f in range(fields):
        load_start(f)

    barrier = pltpu.get_barrier_semaphore()

    def greet_lat(t, carry):
        other = lax.rem(lat + t, n_lat)
        for v in range(2):
            pl.semaphore_signal(
                barrier, inc=1, device_id=(lon, other, (lev, other_lev)[v]), device_id_type=MESH
            )
        return carry

    def greet_lon(t, carry):
        pl.semaphore_signal(
            barrier, inc=1, device_id=(lax.rem(lon + t, n_lon), lat, lev), device_id_type=MESH
        )
        return carry

    pl.semaphore_signal(barrier, inc=1, device_id=(lon, lat, other_lev), device_id_type=MESH)
    lax.fori_loop(1, n_lat, greet_lat, 0)
    lax.fori_loop(1, n_lon, greet_lon, 0)

    lat0 = lat * rows
    lon0 = lon * cols
    n_total = cols * n_lon
    me = (lon * n_lat + lat) * n_lev + lev
    local, obs_row, obs_col = [], [], []
    for b in range(batches):
        owner = owner_ref[b]
        columns = columns_ref[b : b + 1]
        local.append(columns + jnp.where(owner == me, 0, n_total * rows * n_lat))
        obs_row.append(owner // n_lev % n_lat * rows + columns // cols)
        obs_col.append(owner // (n_lat * n_lev) * cols + columns % cols)

    @pl.when(jnp.logical_not(has_up))
    def _():
        for s in range(3):
            state[s, 0:WIDTH] = jnp.zeros((WIDTH, total, cols), jnp.float32)

    @pl.when(jnp.logical_not(has_down))
    def _():
        for s in range(3):
            state[s, rows + WIDTH :] = jnp.zeros((WIDTH, total, cols), jnp.float32)

    load_wait(0)

    picked = None
    for pair in range(rows // 2):
        parts = [state[0, WIDTH + 2 * pair + j, 0:members] for j in range(2)]
        x0 = jnp.concatenate(parts, axis=1)
        hi = x0.astype(jnp.bfloat16)
        rest = x0 - hi.astype(jnp.float32)
        mid, lo = split(rest)
        cell = lax.broadcasted_iota(jnp.int32, (2 * cols, count), 0) + pair * 2 * cols
        hot = [
            jnp.where(cell == local[b], 1.0, 0.0).astype(jnp.bfloat16)
            for b in range(batches)
        ]
        term = dot(jnp.concatenate([hi, mid, lo], axis=0), jnp.concatenate(hot, axis=1))
        picked = term if picked is None else picked + term
    picked = picked[:members] + (picked[members : 2 * members] + picked[2 * members :])
    halves = count // LANES
    for b in range(batches):
        for p in range(n_lat):
            for h in range(halves):
                at = b * count + h * LANES
                cand[b, p, h * per : (h + 1) * per] = picked[p * per : (p + 1) * per, at : at + LANES]

    for f in range(1, fields):
        load_wait(f)
    pl.semaphore_wait(barrier, 2 * n_lat + n_lon - 2)

    def field_slice(c):
        return pl.ds(pl.multiple_of(c * members, 16), members)

    def block(i):
        return pl.ds(pl.multiple_of(i * members, 16), members)

    def lat_copy(section, c, down):
        src = rows if down else WIDTH
        dst = 0 if down else WIDTH + rows
        return pltpu.make_async_remote_copy(
            src_ref=state.at[section, pl.ds(src, WIDTH), field_slice(c)],
            dst_ref=state.at[section, pl.ds(dst, WIDTH), field_slice(c)],
            send_sem=lat_send.at[section, c, int(down)],
            recv_sem=lat_recv.at[section, c, int(down)],
            device_id=(lon, lat + 1 if down else lat - 1, lev),
            device_id_type=MESH,
        )

    def lat_start(section, c):
        @pl.when(has_up)
        def _():
            lat_copy(section, c, False).start()

        @pl.when(has_down)
        def _():
            lat_copy(section, c, True).start()

    def lat_wait(section, c):
        @pl.when(has_up)
        def _():
            lat_copy(section, c, True).wait_recv()

        @pl.when(has_down)
        def _():
            lat_copy(section, c, False).wait_recv()

    def lat_sent(section, c):
        @pl.when(has_up)
        def _():
            lat_copy(section, c, False).wait_send()

        @pl.when(has_down)
        def _():
            lat_copy(section, c, True).wait_send()

    def lon_copy(section, c, to_east):
        return pltpu.make_async_remote_copy(
            src_ref=packed.at[section, field_slice(c)],
            dst_ref=(left_in if to_east else right_in).at[section, field_slice(c)],
            send_sem=lon_send.at[section, c, int(to_east)],
            recv_sem=lon_recv.at[section, c, int(to_east)],
            device_id=(east if to_east else west, lat, lev),
            device_id_type=MESH,
        )

    def wait_all(buf, number, sem):
        view = buf.at[pl.ds(0, number)]
        pltpu.make_async_copy(view, view, sem).wait()

    def piece(other, to_lev, sem):
        pltpu.make_async_remote_copy(
            src_ref=cand.at[to_lev, other], dst_ref=rs_buf.at[lev, lat],
            send_sem=share_send.at[sem], recv_sem=share_recv.at[sem],
            device_id=(lon, other, to_lev), device_id_type=MESH,
        ).start()

    def send_piece(t, carry):
        other = lax.rem(lat + t, n_lat)
        piece(other, lev, 1)
        piece(other, other_lev, 0)
        return carry

    def send_sum(t, carry):
        pltpu.make_async_remote_copy(
            src_ref=z_buf.at[lon], dst_ref=z_buf.at[lon],
            send_sem=share_send.at[2], recv_sem=share_recv.at[2],
            device_id=(lax.rem(lon + t, n_lon), lat, lev), device_id_type=MESH,
        ).start()
        return carry

    def result(other, to_lev, sem):
        pltpu.make_async_remote_copy(
            src_ref=full.at[lev, lat], dst_ref=full.at[lev, lat],
            send_sem=share_send.at[sem], recv_sem=share_recv.at[sem],
            device_id=(lon, other, to_lev), device_id_type=MESH,
        ).start()

    def send_total(t, carry):
        other = lax.rem(lat + t, n_lat)
        result(other, lev, 3)
        result(other, other_lev, 4)
        return carry

    def lon_sq(gap):
        gap = jnp.abs(gap)
        gap = jnp.minimum(gap, n_total - gap) * (1.0 / (n_total // 2))
        return gap * gap

    wide = rows + 2 * WIDTH

    def tapers(first, last):
        def one(n, carry):
            b = n // wide
            i = lax.rem(n, wide)
            here = (lat0 + i - WIDTH).astype(jnp.float32)
            for at in range(0, count, 64):
                sl = pl.ds(at, 64)
                dlat = (here - row_part[b, sl]) * (1.0 / (2.0 * rows))
                taper_buf[b, i, sl] = taper_of(dlat * dlat + lon_part[b, sl])
            return carry

        lax.fori_loop(first, last, one, 0)

    piece(lat, other_lev, 0)
    lax.fori_loop(1, n_lat, send_piece, 0)
    lat_start(0, 0)
    rs_buf[lev, lat] = cand[lev, lat]
    for b in range(batches):
        grid_cols = (lon0 + lax.broadcasted_iota(jnp.int32, (count, cols), 1)).astype(jnp.float32)
        wide_col = jnp.broadcast_to(obs_col[b].astype(jnp.float32), (cols, count)).T
        col_part[b] = wide_col
        lon_part[b] = lon_sq(grid_cols - wide_col)
        row_part[b] = jnp.broadcast_to(obs_row[b].astype(jnp.float32), (cols, count)).T
    tapers(0, 16)
    wait_all(rs_buf.at[lev], n_lat - 1, share_recv.at[1])
    wait_all(rs_buf.at[other_lev], n_lat, share_recv.at[0])
    z_buf[lon] = jnp.sum(rs_buf[0], axis=0) + jnp.sum(rs_buf[1], axis=0)
    lax.fori_loop(1, n_lon, send_sum, 0)
    lat_start(0, 1)
    tapers(16, 28)
    wait_all(z_buf, n_lon - 1, share_recv.at[2])
    full[lev, lat] = jnp.sum(z_buf[...], axis=0)
    result(lat, other_lev, 4)
    lax.fori_loop(1, n_lat, send_total, 0)
    lat_start(0, 2)
    tapers(28, 2 * wide)

    for r in range(rows):
        for d in range(2):
            c = jnp.broadcast_to(cour_ref[d, r : r + 1], (SUB, cols))
            up = jnp.maximum(c, 0.0) * (-1.0 / 60.0)
            dn = jnp.minimum(c, 0.0) * (-1.0 / 60.0)
            if d == 0:
                coef[r, 0] = up
                coef[r, 1] = dn
            else:
                for o in range(7):
                    w = PLUS_WEIGHTS[o] * up if o < 6 else jnp.zeros_like(c)
                    if o > 0:
                        w = w + MINUS_WEIGHTS[o - 1] * dn
                    coef[r, 2 + o] = w

    k = lax.broadcasted_iota(jnp.int32, (4 * cols, cols), 0)
    j = lax.broadcasted_iota(jnp.int32, (4 * cols, cols), 1)
    kk = lax.rem(k, cols)
    side = lax.rem(kk, slot)
    halo_col = jnp.where(side < WIDTH, side - WIDTH, cols + side - WIDTH)
    gap = jnp.where(k < 2 * cols, kk, halo_col) - j
    for first, weights, lane0 in ((-3, PLUS_WEIGHTS, 0), (-2, MINUS_WEIGHTS, cols)):
        w = jnp.zeros((4 * cols, cols), jnp.float32)
        for n in range(6):
            w = jnp.where(gap == first + n, weights[n], w)
        stencil[:, lane0 : lane0 + cols] = w.astype(jnp.bfloat16)
    side = lax.rem(j, slot)[: 2 * cols]
    wanted = jnp.where(side < WIDTH, cols - WIDTH + side, side - WIDTH)
    hit = (wanted == kk[: 2 * cols]) & (j[: 2 * cols] < slot * rows)
    picker[...] = jnp.where(hit, 1.0, 0.0).astype(jnp.bfloat16)

    lane = lax.broadcasted_iota(jnp.int32, (members, cols), 1)
    from_left = lax.rem(lane, slot) < WIDTH
    slot_of = lane // slot
    for r in range(rows):
        slot_mask[r] = jnp.where(slot_of == r, 1.0, 0.0).astype(jnp.bfloat16)

    wait_all(full.at[lev], n_lat - 1, share_recv.at[3])
    wait_all(full.at[other_lev], n_lat, share_recv.at[4])
    for b in range(batches):
        for p in range(n_lat):
            for h in range(halves):
                at = h * LANES
                prior_buf[b, p * per : (p + 1) * per, at : at + LANES] = full[
                    b, p, h * per : (h + 1) * per
                ]

    prior = prior_buf[0]
    for b in range(batches):
        spread, gain = innovation(prior, value_ref[b : b + 1], err_ref[b : b + 1])
        s_op[b] = spread_operand(spread)
        ghi, glo = split(gain)
        g_op[b] = jnp.concatenate([ghi, glo], axis=0)
        if b + 1 < batches:
            prior = prior_buf[b + 1]
            both = [jnp.concatenate([v[b]] * halves, axis=1) for v in (row_part, col_part)]
            dlat = (obs_row[b + 1].astype(jnp.float32) - both[0]) * (1.0 / (2.0 * rows))
            taper = taper_of(dlat * dlat + lon_sq(obs_col[b + 1].astype(jnp.float32) - both[1]))
            cov = dot(s_op[b], anomaly_operand(prior))
            prior = prior + apply_gain(g_op[b], ghi, taper * cov)

    def assimilate(c):
        def step(n, carry):
            at = [n * STEP + j for j in range(STEP)]
            x = [state[0, i, field_slice(c)] for i in at]
            for b in range(batches):
                operand = jnp.concatenate([anomaly_operand(v) for v in x], axis=1)
                cov = dot(s_op[b], operand)
                weighted = jnp.concatenate(
                    [
                        taper_buf[b, i] * cov[:, j * cols : (j + 1) * cols]
                        for j, i in enumerate(at)
                    ],
                    axis=1,
                )
                change = apply_gain(g_op[b], g_op[b, :members], weighted)
                x = [v + change[:, j * cols : (j + 1) * cols] for j, v in enumerate(x)]
            for i, v in zip(at, x):
                state[0, i, field_slice(c)] = v
                hi, lo = split(v)
                lhs[c, block(i), 0:cols] = hi
                lhs[c, block(i), cols : 2 * cols] = lo
            return carry

        lax.fori_loop(0, wide // STEP, step, 0)


    def lon_start(section, c):
        def step(n, acc):
            at = pl.multiple_of((WIDTH + n * PACK_SPAN) * members, 16)
            got = dot(lhs[c, pl.ds(at, PACK_SPAN * members), 0 : 2 * cols], picker[...])
            for m in range(PACK_SPAN):
                acc = jnp.where(slot_of == n * PACK_SPAN + m, got[m * members : (m + 1) * members], acc)
            return acc

        zero = jnp.zeros((members, cols), jnp.float32)
        packed[section, field_slice(c)] = lax.fori_loop(0, rows // PACK_SPAN, step, zero)
        lon_copy(section, c, True).start()
        lon_copy(section, c, False).start()

    def lon_finish(section, c):
        lon_copy(section, c, True).wait_recv()
        lon_copy(section, c, False).wait_recv()
        halo = jnp.where(
            from_left, left_in[section, field_slice(c)], right_in[section, field_slice(c)]
        )

        parts = split(halo)

        def step(n, carry):
            for m in range(SUM_SPAN):
                r = n * SUM_SPAN + m
                for p in range(2):
                    lanes = slice((2 + p) * cols, (3 + p) * cols)
                    lhs[c, block(WIDTH + r), lanes] = parts[p] * slot_mask[r]
            at = pl.multiple_of((WIDTH + n * SUM_SPAN) * members, 16)
            to = pl.multiple_of(n * SUM_SPAN * members, 16)
            rows_in = pl.ds(at, SUM_SPAN * members)
            dpm[pl.ds(to, SUM_SPAN * members)] = dot(lhs[c, rows_in], stencil[...])
            return carry

        lax.fori_loop(0, rows // SUM_SPAN, step, 0)

    def do_rows(section, c, first, stop):
        scale = (1.0 / 3.0, 0.5, 1.0)[section]

        def do_row(n, carry):
            r = n if isinstance(first, int) else first(n)
            w = [jnp.concatenate([coef[r, o]] * 2, axis=0) for o in range(9)]
            for g in range(members // (2 * SUB)):
                off = g * 2 * SUB
                sl = pl.ds(pl.multiple_of(c * members + off, 2 * SUB), 2 * SUB)
                at = pl.ds(pl.multiple_of(r * members + off, 2 * SUB), 2 * SUB)
                q = state[section, WIDTH + r, sl]
                t = w[0] * dpm[at, 0:cols]
                u = w[1] * dpm[at, cols : 2 * cols] + w[5] * q
                for o in (1, 2, 3):
                    t = t + w[5 - o] * state[section, WIDTH + r - o, sl]
                    u = u + w[5 + o] * state[section, WIDTH + r + o, sl]
                base = q if section == 0 else state[0, WIDTH + r, sl]
                if section < 2:
                    value = base + (t + u) * scale
                    state[section + 1, WIDTH + r, sl] = value
                    hi, lo = split(value)
                    to = pl.ds(pl.multiple_of((WIDTH + r) * members + off, 2 * SUB), 2 * SUB)
                    lhs[c, to, 0:cols] = hi
                    lhs[c, to, cols : 2 * cols] = lo
                else:
                    at = (off * fields + c) * rows + r
                    out_ref[pl.ds(at, 2 * SUB, stride=fields * rows), :] = base + (t + u)
            return carry

        lax.fori_loop(first if isinstance(first, int) else 0, stop, do_row, 0)

    def interior(section, c):
        do_rows(section, c, WIDTH, rows - WIDTH)

    def edges(section, c):
        def edge_row(n):
            return jnp.where(n < WIDTH, n, n + rows - 2 * WIDTH)

        do_rows(section, c, edge_row, 2 * WIDTH)

    def first_pass(c, carry):
        @pl.when(c < fields)
        def _():
            lat_wait(0, c)
            lat_sent(0, c)
            assimilate(c)
            lon_start(0, c)

        @pl.when(c > 0)
        def _():
            lon_finish(0, c - 1)
            edges(0, c - 1)
            lat_start(1, c - 1)
            interior(0, c - 1)
            lon_start(1, c - 1)

        return carry

    lax.fori_loop(0, fields + 1, first_pass, 0)

    for section in (1, 2):

        def later_pass(c, carry):
            lon_finish(section, c)
            interior(section, c)
            lat_wait(section, c)
            edges(section, c)
            if section < 2:
                lat_start(section + 1, c)
                lon_start(section + 1, c)
            return carry

        lax.fori_loop(0, fields, later_pass, 0)

    wait_all(rs_buf.at[lev], n_lat - 1, share_send.at[1])
    wait_all(rs_buf.at[other_lev], n_lat, share_send.at[0])
    wait_all(z_buf, n_lon - 1, share_send.at[2])
    wait_all(full.at[lev], n_lat - 1, share_send.at[3])
    wait_all(full.at[other_lev], n_lat, share_send.at[4])
    for section in range(3):
        for c in range(fields):
            lon_copy(section, c, True).wait_send()
            lon_copy(section, c, False).wait_send()
            if section > 0:
                lat_sent(section, c)


def on_device(ensemble, courant, obs_value, obs_error, owner_device, columns):
    members, fields, _, rows, cols = ensemble.shape
    dims = tuple(lax.axis_size(a) for a in ("lon", "lat", "lev"))
    n_lon, n_lat, _ = dims
    batches, count = columns.shape
    total = fields * members
    piece = (members // n_lat * count // LANES, LANES)
    f32, bf16 = jnp.float32, jnp.bfloat16
    vmem = pl.BlockSpec(memory_space=pltpu.VMEM)
    smem = pl.BlockSpec(memory_space=pltpu.SMEM)
    dma = pltpu.SemaphoreType.DMA
    out = pl.pallas_call(
        functools.partial(kernel, dims),
        out_shape=jax.ShapeDtypeStruct((members * fields * rows, cols), f32),
        in_specs=[pl.BlockSpec(memory_space=pl.ANY)] + [vmem] * 3 + [smem, vmem],
        out_specs=vmem,
        scratch_shapes=[
            pltpu.VMEM((batches, n_lat) + piece, f32),
            pltpu.VMEM((batches, n_lat) + piece, f32),
            pltpu.VMEM((n_lon,) + piece, f32),
            pltpu.VMEM((batches, n_lat) + piece, f32),
            pltpu.VMEM((batches, members, count), f32),
            pltpu.VMEM((batches, count, 256), bf16),
            pltpu.VMEM((batches, 2 * members, count), bf16),
            pltpu.VMEM((batches, count, cols), f32),
            pltpu.VMEM((batches, count, cols), f32),
            pltpu.VMEM((batches, count, cols), f32),
            pltpu.VMEM((batches, rows + 2 * WIDTH, count, cols), f32),
            pltpu.VMEM((3, rows + 2 * WIDTH, total, cols), f32),
            pltpu.VMEM((3, total, cols), f32),
            pltpu.VMEM((3, total, cols), f32),
            pltpu.VMEM((3, total, cols), f32),
            pltpu.VMEM((fields, (rows + 2 * WIDTH) * members, 4 * cols), bf16),
            pltpu.VMEM((rows * members, 2 * cols), f32),
            pltpu.VMEM((rows, 9, SUB, cols), f32),
            pltpu.VMEM((4 * cols, 2 * cols), bf16),
            pltpu.VMEM((2 * cols, cols), bf16),
            pltpu.VMEM((rows, members, cols), bf16),
            dma((fields,)),
            dma((5,)),
            dma((5,)),
            dma((3, fields, 2)),
            dma((3, fields, 2)),
            dma((3, fields, 2)),
            dma((3, fields, 2)),
        ],
        compiler_params=pltpu.CompilerParams(
            has_side_effects=True, collective_id=0, vmem_limit_bytes=VMEM_LIMIT
        ),
        name="filter_and_advect",
    )(
        ensemble, courant[:, 0], obs_value, obs_error, owner_device, columns,
    )
    return out.reshape(ensemble.shape)


def solution(mesh):
    return jax.shard_map(
        on_device,
        mesh=mesh,
        in_specs=(
            P(None, None, "lev", "lat", "lon"),
            P(None, "lev", "lat", "lon"),
            P(),
            P(),
            P(),
            P(),
        ),
        out_specs=P(None, None, "lev", "lat", "lon"),
        check_vma=False,
    )
```

time: 76.5 us -> 60.9 us (0.80)
  the two profiles are of different devices: /device:TPU:1 before, /device:TPU:8 now
where the time goes in v3:
time: 60.9 us; the launch traced here: 60.7 us
  Pallas kernels  57.7 us (95%)
  local copies, waits for them, and re-layouts  2.94 us (5%)
    pallas_call x1, Pallas kernels, on_device(): pl.pallas_call(functools.partial(kernel, dims), out_shape=jax.ShapeDtypeS...  57.7 us
    unnamed x1, local copies, waits for them, and re-layouts  2.94 us

profile of v3, /device:TPU:8, one launch (start us, length us, event | category | flops | bytes accessed | tf_op | source)
XLA Modules:
  0.0 60.7 jit_solution(3636690466328711623)
XLA Ops:
  0.0 57.7 %filter_and_advect.1 = f32[3840,128]{1,0:T(8,128)} custom-call(f32[80,3,1,16,128]{4,3,2,1,0:T(8,128)} %x_ref.1, f32[2,16,128]{2,1,0:T(8,128)} %bitcast.5, f32[2,256]{1,0:T(2,128)} %value_ref.1, f32[2,256]{1,0:T(2,128)} %err_ref.1, s32[2]{0:T(128)} %owner_ref.1, s32[2,256]{1,0:T(2,128)} %columns_ref.1), custom_call_target="tpu_custom_call" | custom-call | tf_op jit(solution)/shard_map/filter_and_advect/pallas_call | solution.py:549
  57.7 2.9 %copy.9 = f32[80,3,1,16,128]{4,3,2,1,0:T(8,128)} copy(f32[80,3,1,16,128]{4,3,2,1,0:T(8,128)} %bitcast.4) | data formatting | bytes 3932160

commit v4 on v3

--- a/solution.py
+++ b/solution.py
@@ -13,7 +13,7 @@
 VMEM_LIMIT = 60 * 1024 * 1024
 WIDTH = 3
 SUB = 8
-STEP = 11
+STEP = 22
 SUM_SPAN = 16
 PACK_SPAN = 16
 LANES = 128

time: 60.9 us -> 60.2 us (0.989)
  Pallas kernels: 57.7 us -> 57 us
    pallas_call x1, Pallas kernels: 57.7 us -> 57 us  [on_device(): pl.pallas_call(functools.partial(kernel, dims), out_shape=jax.ShapeDtypeS...]
where the time goes in v4:
time: 60.2 us; the launch traced here: 60 us
  Pallas kernels  57 us (95%)
  local copies, waits for them, and re-layouts  2.94 us (5%)
    pallas_call x1, Pallas kernels, on_device(): pl.pallas_call(functools.partial(kernel, dims), out_shape=jax.ShapeDtypeS...  57 us
    unnamed x1, local copies, waits for them, and re-layouts  2.94 us

profile of v4, /device:TPU:8, one launch (start us, length us, event | category | flops | bytes accessed | tf_op | source)
XLA Modules:
  0.0 60.0 jit_solution(11064146434611898998)
XLA Ops:
  0.0 57.0 %filter_and_advect.1 = f32[3840,128]{1,0:T(8,128)} custom-call(f32[80,3,1,16,128]{4,3,2,1,0:T(8,128)} %x_ref.1, f32[2,16,128]{2,1,0:T(8,128)} %bitcast.5, f32[2,256]{1,0:T(2,128)} %value_ref.1, f32[2,256]{1,0:T(2,128)} %err_ref.1, s32[2]{0:T(128)} %owner_ref.1, s32[2,256]{1,0:T(2,128)} %columns_ref.1), custom_call_target="tpu_custom_call" | custom-call | tf_op jit(solution)/shard_map/filter_and_advect/pallas_call | solution.py:549
  57.0 2.9 %copy.9 = f32[80,3,1,16,128]{4,3,2,1,0:T(8,128)} copy(f32[80,3,1,16,128]{4,3,2,1,0:T(8,128)} %bitcast.4) | data formatting | bytes 3932160

commit v5 on v4

--- a/solution.py
+++ b/solution.py
@@ -82,8 +82,8 @@
     x_ref, cour_ref, value_ref, err_ref, owner_ref, columns_ref, out_ref,
     cand, rs_buf, z_buf, full, prior_buf,
     s_op, g_op, lon_part, row_part, col_part, taper_buf,
-    state, packed, left_in, right_in, lhs, dpm, coef, stencil, picker, slot_mask,
-    load_sem, share_send, share_recv, lat_send, lat_recv, lon_send, lon_recv,
+    state, packed, left_in, right_in, lhs, dpm, coef, stencil, picker, slot_mask, result_buf,
+    load_sem, store_sem, share_send, share_recv, lat_send, lat_recv, lon_send, lon_recv,
 ):
     n_lon, n_lat, n_lev = dims
     members, fields, _, rows, cols = x_ref.shape
@@ -473,11 +473,22 @@
                     lhs[c, to, 0:cols] = hi
                     lhs[c, to, cols : 2 * cols] = lo
                 else:
-                    at = (off * fields + c) * rows + r
-                    out_ref[pl.ds(at, 2 * SUB, stride=fields * rows), :] = base + (t + u)
+                    result_buf[r, sl] = base + (t + u)
             return carry
 
         lax.fori_loop(first if isinstance(first, int) else 0, stop, do_row, 0)
+
+    def store_row(c, r):
+        pltpu.make_async_copy(
+            result_buf.at[r, field_slice(c)], x_out(c, r), store_sem.at[c]
+        ).start()
+
+    def x_out(c, r):
+        return out_ref.at[:, c, 0, r]
+
+    def store_wait(c):
+        view = result_buf.at[:, field_slice(c)]
+        pltpu.make_async_copy(view, view, store_sem.at[c]).wait()
 
     def interior(section, c):
         do_rows(section, c, WIDTH, rows - WIDTH)
@@ -513,8 +524,14 @@
         def later_pass(c, carry):
             lon_finish(section, c)
             interior(section, c)
+            if section == 2:
+                for r in range(WIDTH, rows - WIDTH):
+                    store_row(c, r)
             lat_wait(section, c)
             edges(section, c)
+            if section == 2:
+                for r in list(range(WIDTH)) + list(range(rows - WIDTH, rows)):
+                    store_row(c, r)
             if section < 2:
                 lat_start(section + 1, c)
                 lon_start(section + 1, c)
@@ -522,6 +539,8 @@
 
         lax.fori_loop(0, fields, later_pass, 0)
 
+    for c in range(fields):
+        store_wait(c)
     wait_all(rs_buf.at[lev], n_lat - 1, share_send.at[1])
     wait_all(rs_buf.at[other_lev], n_lat, share_send.at[0])
     wait_all(z_buf, n_lon - 1, share_send.at[2])
@@ -548,9 +567,9 @@
     dma = pltpu.SemaphoreType.DMA
     out = pl.pallas_call(
         functools.partial(kernel, dims),
-        out_shape=jax.ShapeDtypeStruct((members * fields * rows, cols), f32),
+        out_shape=jax.ShapeDtypeStruct(ensemble.shape, f32),
         in_specs=[pl.BlockSpec(memory_space=pl.ANY)] + [vmem] * 3 + [smem, vmem],
-        out_specs=vmem,
+        out_specs=pl.BlockSpec(memory_space=pl.ANY),
         scratch_shapes=[
             pltpu.VMEM((batches, n_lat) + piece, f32),
             pltpu.VMEM((batches, n_lat) + piece, f32),
@@ -573,6 +592,8 @@
             pltpu.VMEM((4 * cols, 2 * cols), bf16),
             pltpu.VMEM((2 * cols, cols), bf16),
             pltpu.VMEM((rows, members, cols), bf16),
+            pltpu.VMEM((rows, total, cols), f32),
+            dma((fields,)),
             dma((fields,)),
             dma((5,)),
             dma((5,)),
@@ -588,7 +609,7 @@
     )(
         ensemble, courant[:, 0], obs_value, obs_error, owner_device, columns,
     )
-    return out.reshape(ensemble.shape)
+    return out
 
 
 def solution(mesh):

time: 60.2 us -> 59.7 us (level)
  no operation moved by 1% of the time
where the time goes in v5:
time: 59.7 us; the launch traced here: 59.4 us
  Pallas kernels  56.5 us (95%)
  local copies, waits for them, and re-layouts  2.94 us (5%)
    pallas_call x1, Pallas kernels, on_device(): pl.pallas_call(functools.partial(kernel, dims), out_shape=jax.ShapeDtypeS...  56.5 us
    unnamed x1, local copies, waits for them, and re-layouts  2.94 us

profile of v5, /device:TPU:8, one launch (start us, length us, event | category | flops | bytes accessed | tf_op | source)
XLA Modules:
  0.0 59.4 jit_solution(17307199560687508705)
XLA Ops:
  0.0 56.5 %filter_and_advect.1 = f32[80,3,1,16,128]{4,3,2,1,0:T(8,128)} custom-call(f32[80,3,1,16,128]{4,3,2,1,0:T(8,128)} %x_ref.1, f32[2,16,128]{2,1,0:T(8,128)} %bitcast.1, f32[2,256]{1,0:T(2,128)} %value_ref.1, f32[2,256]{1,0:T(2,128)} %err_ref.1, s32[2]{0:T(128)} %owner_ref.1, s32[2,256]{1,0:T(2,128)} %columns_ref.1), custom_call_target="tpu_custom_call" | custom-call | tf_op jit(solution)/shard_map/filter_and_advect/pallas_call | solution.py:568
  56.5 2.9 %copy.8 = f32[80,3,1,16,128]{4,3,2,1,0:T(8,128)} copy(f32[80,3,1,16,128]{4,3,2,1,0:T(8,128)} %filter_and_advect.1) | data formatting | bytes 3932160
